TPU v7x, 512 devices: a whole 4x8x8 slice. The times are simulated.
512 devices in a mesh: dp: 16 (over z_hi, x, core), shard: 32 (over y, z_lo).
Axes of the slice: x: 4, y: 8, z: 8 (z_hi: 2, z_lo: 4; z = z_hi * 4 + z_lo), core: 2. Of those that a mesh axis runs over, the one named last changes fastest.
Arguments:
- grad_groups: bfloat16 [16, 106496, 256], P('dp', 'shard'), may hold values from -9 to 9
- master: float32 [106496, 256], P(('shard', 'dp')), may hold values from -0.75 to 0.75
- moment1: float32 [106496, 256], P(('shard', 'dp')), may hold values from -0.75 to 0.75
- moment2: float32 [106496, 256], P(('shard', 'dp')), may hold values from 0.001 to 0.1
- proj: bfloat16 [256, 4096], P('dp'), may hold values from -1 to 1
- ln_gain: float32 [4096], replicated, may hold values from 0.25 to 1.75
- w_qkv: bfloat16 [4096, 6144], P('dp', 'shard'), may hold values from -0.09375 to 0.09375
- token_owner: int32 [65536, 1], P(('dp', 'shard')), may hold values from 0 to 31; in each aligned block of 128 rows (0 to 127, 128 to 255, ...) at most 8 rows name the same one
- token_row: int32 [65536], P(('dp', 'shard')), may hold values from 0 to 207
Outputs:
- new_master: float32 [106496, 256], P(('shard', 'dp'))
- new_moment1: float32 [106496, 256], P(('shard', 'dp'))
- new_moment2: float32 [106496, 256], P(('shard', 'dp'))
- qkv: bfloat16 [65536, 6144], P('dp', 'shard')
Inputs may be any that keep to these rules, and one draw needn't show every extreme that they name: `token_owner`: of the 128 tokens of one device at most 8 name any one shard block, and some block of every device is named by exactly 8; so at most 1 token of one device fall on one owner of one block, and some owner receives exactly 1 from every device.
All inputs are finite; a program needn't handle non-finite values.
Results may differ from a plain program's by a relative error of at most 0.018.
Values may be sent and summed in bfloat16 or wider, within the bound.
A program may use at most 64 MiB of HBM per device.

v0:
```python
import math

import jax
import jax.numpy as jnp
from jax import lax
from jax.sharding import PartitionSpec as P


def adam_step(summed, master, moment1, moment2, clip_factor):
    grad = clip_factor * summed
    new_moment1 = 0.9 * moment1 + 0.1 * grad
    new_moment2 = 0.95 * moment2 + 0.05 * grad * grad
    fixed_one = new_moment1 / (1.0 - 0.9**10)
    fixed_two = new_moment2 / (1.0 - 0.95**10)
    new_master = master - 0.01 * (fixed_one / (jnp.sqrt(fixed_two) + 1e-08) + 0.1 * master)
    return (new_master, new_moment1, new_moment2)


def fetch_weights(proj, w_qkv):
    return (
        lax.all_gather(proj, "dp", axis=0, tiled=True),
        lax.all_gather(w_qkv, "dp", axis=0, tiled=True),
    )


def body(grad_groups, master, moment1, moment2, proj, ln_gain, w_qkv, token_owner, token_row):
    summed = lax.psum_scatter(
        grad_groups[0].astype(jnp.float32).astype(jnp.bfloat16),
        "dp",
        scatter_dimension=0,
        tiled=True,
    ).astype(jnp.float32)
    total = lax.psum(jnp.sum(summed * summed), ("dp", "shard"))
    entries = summed.shape[0] * summed.shape[1] * lax.axis_size("dp") * lax.axis_size("shard")
    clip_factor = jnp.minimum(1.0, 0.2 * math.sqrt(entries) / (jnp.sqrt(total) + 1e-06))
    new_master, new_moment1, new_moment2 = adam_step(summed, master, moment1, moment2, clip_factor)
    table = new_master.astype(jnp.bfloat16)
    shards = lax.axis_size("shard")
    groups = lax.axis_size("dp")
    tok_count = token_row.shape[0]
    capacity = max(2, 2 * tok_count // shards)
    owner = token_owner[:, 0]
    member = (owner[:, None] == jnp.arange(shards, dtype=jnp.int32)[None, :]).astype(jnp.int32)
    places = jnp.cumsum(member, axis=0) - 1
    slot = jnp.sum(places * member, axis=1)
    target = owner * capacity + slot
    wanted = jnp.zeros((shards * capacity,), jnp.int32).at[target].set(token_row + 1)
    arrived = lax.all_to_all(
        wanted.reshape(shards, capacity), "shard", split_axis=0, concat_axis=0, tiled=True
    )
    sender = jnp.arange(shards, dtype=jnp.int32)[:, None]
    owned = table.shape[0]
    block = lax.all_gather(table, "dp", axis=0, tiled=True)
    columns = jnp.arange(capacity, dtype=jnp.int32)[None, :]
    index = (columns + sender) % groups * owned + jnp.maximum(arrived - 1, 0)
    picked = block[index]
    looked = jnp.where((arrived > 0)[:, :, None], picked, jnp.zeros_like(picked))
    returned = lax.all_to_all(looked, "shard", split_axis=0, concat_axis=0, tiled=True)
    own_rows = returned.reshape(shards * capacity, returned.shape[2])[target]
    group_rows = lax.all_gather(own_rows, "shard", axis=0, tiled=True)
    proj_full, w_full = fetch_weights(proj, w_qkv)
    proj_float = proj_full.astype(jnp.float32)
    gram = jnp.dot(proj_float, proj_float.T, precision=lax.Precision.HIGHEST)
    folded = jnp.dot(
        proj_float * ln_gain[None, :], w_full.astype(jnp.float32), precision=lax.Precision.HIGHEST
    )
    rows_float = group_rows.astype(jnp.float32)
    width = proj_full.shape[1]
    mean_sq = (
        jnp.sum(jnp.dot(rows_float, gram, precision=lax.Precision.HIGHEST) * rows_float, axis=1)
        / width
    )
    values = jnp.dot(rows_float, folded, precision=lax.Precision.HIGHEST)
    qkv = (values * lax.rsqrt(mean_sq + 1e-05)[:, None]).astype(jnp.bfloat16)
    return (new_master, new_moment1, new_moment2, qkv)


def solution(mesh):
    placed = (
        P("dp", "shard", None),
        P(("shard", "dp"), None),
        P(("shard", "dp"), None),
        P(("shard", "dp"), None),
        P("dp", None),
        P(),
        P("dp", "shard"),
        P(("dp", "shard"), None),
        P(("dp", "shard")),
    )
    return jax.shard_map(
        body,
        mesh=mesh,
        in_specs=placed,
        out_specs=(
            P(("shard", "dp"), None),
            P(("shard", "dp"), None),
            P(("shard", "dp"), None),
            P("dp", "shard"),
        ),
        check_vma=False,
    )
```

profile of v0, /device:TPU:6, one launch (start us, length us, event | category | flops | bytes accessed | tf_op | source)
XLA Modules:
  0.0 552.6 jit_solution(11939765284829291614)
XLA Ops:
  7.2 0.7 reduce-scatter.2.cloned.1.call-update
  8.0 102.8 %reduce-scatter.2.cloned.1.call-done = bf16[208,256]{1,0:T(8,128)(2,1)} async-done(((bf16[3328,256]{1,0:T(8,128)(2,1)}), bf16[208,256]{1,0:T(8,128)(2,1)}) %reduce-scatter.2.cloned.1.call-update) | async-done | bytes 106512 | tf_op jit(solution)/shard_map/reduce_scatter | solution.py:27
  110.8 1.6 fusion.8
  112.4 94.3 %psum.7 = f32[]{:T(128)} all-reduce(f32[]{:T(128)} %fusion.8), channel_id=1, replica_groups=mesh['dp'=16,'shard'=32] {'dp','shard'}, use_global_device_ids=true, to_apply=%region_2.0 | all-reduce | flops 1 | bytes 8 | tf_op jit(solution)/shard_map/psum | solution.py:33
  207.4 2.2 fusion.20
  209.6 0.7 all-gather.10.cloned.1.call-update
  210.4 0.5 all-gather.8.cloned.1.call-update
  211.0 0.2 reduce_window_sum.11
  211.4 1.0 scatter_custom_fusion
  212.5 17.0 %all_to_all.14 = s32[32,1,8]{2,1,0:T(1,128)S(1)} all-to-all(s32[32,1,8]{2,1,0:T(1,128)S(1)} %bitcast.28), channel_id=1, replica_groups=mesh['dp'=16,'shard'=32] {'shard'}, dimensions={0} | all-to-all | bytes 2048 | tf_op jit(solution)/shard_map/all_to_all | solution.py:48
  229.8 42.6 %all-gather.6.cloned.1.call-done = bf16[3328,256]{1,0:T(8,128)(2,1)} async-done(((bf16[208,256]{1,0:T(8,128)(2,1)}), bf16[3328,256]{1,0:T(8,128)(2,1)}) %all-gather.6.cloned.1.call-update) | async-done | bytes 1703952 | tf_op jit(solution)/shard_map/all_gather | solution.py:53
  272.5 2.6 gather_fusion
  275.1 0.8 bitcast_select_fusion
  275.9 7.6 %all-to-all-start.1 = ((bf16[32,8,256]{2,1,0:T(8,128)(2,1)}), bf16[32,8,256]{2,1,0:T(8,128)(2,1)S(1)}, u32[]{:S(2)}, u32[]{:S(2)}) async-start(bf16[32,8,256]{2,1,0:T(8,128)(2,1)} %bitcast_select_fusion), calls=%async_computation.2 | async-start | bytes 262144 | tf_op jit(solution)/shard_map/all_to_all | solution.py:58
  283.5 11.4 %all-to-all-done.1 = bf16[32,8,256]{2,1,0:T(8,128)(2,1)S(1)} async-done(((bf16[32,8,256]{2,1,0:T(8,128)(2,1)}), bf16[32,8,256]{2,1,0:T(8,128)(2,1)S(1)}, u32[]{:S(2)}, u32[]{:S(2)}) %all-to-all-start.1) | async-done | bytes 131104 | tf_op jit(solution)/shard_map/all_to_all | solution.py:58
  294.9 0.8 gather_fusion.1
  295.8 0.7 copy.22
  296.5 40.7 %all-gather.10.cloned.1.call-done = bf16[4096,192]{0,1:T(8,128)(2,1)} async-done(((bf16[256,192]{0,1:T(8,128)(2,1)}), bf16[4096,192]{0,1:T(8,128)(2,1)}) %all-gather.10.cloned.1.call-update) | async-done | bytes 1572880 | tf_op jit(solution)/shard_map/all_gather | solution.py:22
  337.2 68.1 %all-gather.8.cloned.1.call-done = bf16[256,4096]{1,0:T(8,128)(2,1)} async-done(((bf16[16,4096]{1,0:T(8,128)(2,1)}), bf16[256,4096]{1,0:T(8,128)(2,1)}) %all-gather.8.cloned.1.call-update) | async-done | bytes 2097168 | tf_op jit(solution)/shard_map/all_gather | solution.py:21
  405.3 4.9 fusion.1
  410.2 0.7 fusion.23
  410.9 128.0 %all-gather.12.cloned.1.call-done = bf16[4096,256]{0,1:T(8,128)(2,1)} async-done(((bf16[128,256]{0,1:T(8,128)(2,1)}), bf16[4096,256]{0,1:T(8,128)(2,1)}) %all-gather.12.cloned.1.call-update) | async-done | bytes 2097168 | tf_op jit(solution)/shard_map/all_gather | solution.py:60
  539.0 4.5 fusion.5
  543.5 2.6 fusion
  (31 shorter events, 1.0 us)
Async XLA Ops:
  7.2 203.7 %copy-start.2 = (s32[128,1]{0,1:T(1,128)S(1)}, s32[128,1]{0,1:T(1,128)}, u32[]{:S(2)}) copy-start(s32[128,1]{0,1:T(1,128)} %param.16) | copy-start | bytes 1540
  7.2 204.2 %copy-start.4 = (s32[128]{0:T(128)S(1)}, s32[128]{0:T(128)}, u32[]{:S(2)}) copy-start(s32[128]{0:T(128)} %param.17) | copy-start | bytes 1540
  7.2 103.6 %reduce-scatter.2.cloned.1.call-start = ((), (), s32[]{:S(2)}) async-start(), calls=%async_computation.3 | async-start | bytes 1810432 | tf_op jit(solution)/shard_map/reduce_scatter | solution.py:27
  7.9 264.5 %all-gather.6.cloned.1.call-start = ((), (), s32[]{:S(2)}) async-start(), calls=%async_computation.4 | async-start | bytes 1810432 | tf_op jit(solution)/shard_map/all_gather | solution.py:53
  207.4 197.9 %copy-start.3 = (f32[4096]{0:T(1024)S(1)}, f32[4096]{0:T(1024)}, u32[]{:S(2)}) copy-start(f32[4096]{0:T(1024)} %param.14) | copy-start | bytes 49156
  209.6 127.6 %all-gather.10.cloned.1.call-start = ((), (), s32[]{:S(2)}) async-start(), calls=%async_computation.6 | async-start | bytes 1671168 | tf_op jit(solution)/shard_map/all_gather | solution.py:22
  210.3 195.0 %all-gather.8.cloned.1.call-start = ((), (), s32[]{:S(2)}) async-start(), calls=%async_computation.5 | async-start | bytes 2228224 | tf_op jit(solution)/shard_map/all_gather | solution.py:21
  275.9 19.1 %all-to-all-start.1 = ((bf16[32,8,256]{2,1,0:T(8,128)(2,1)}), bf16[32,8,256]{2,1,0:T(8,128)(2,1)S(1)}, u32[]{:S(2)}, u32[]{:S(2)}) async-start(bf16[32,8,256]{2,1,0:T(8,128)(2,1)} %bitcast_select_fusion), calls=%async_computation.2 | async-start | bytes 262144 | tf_op jit(solution)/shard_map/all_to_all | solution.py:58
  283.5 255.5 %all-gather.12.cloned.1.call-start = ((), (), s32[]{:S(2)}) async-start(), calls=%async_computation.7 | async-start | bytes 2162688 | tf_op jit(solution)/shard_map/all_gather | solution.py:60
  405.3 4.9 copy-start
  539.0 4.5 copy-start.1
Sparse Core Ops, SparseCore 0:
  12.8 97.9 reduce-scatter.1
  209.7 62.6 all-gather.5
  276.1 61.0 all-gather.9
  340.9 64.3 all-gather.7
  407.9 130.9 all-gather.11
where the time goes:
time: 554 us; the launch traced here: 553 us
  waiting for transfers between devices  396 us (71%)
  blocking collectives  111 us (20%)
  between operations  14.7 us (3%)
  matrix products  12.7 us (2%)
  starting transfers between devices  7.8 us (1%)
  local copies, waits for them, and re-layouts  5.62 us (1%)
    all_gather x1, waiting for transfers between devices, body(): group_rows = lax.all_gather(own_rows, 'shard', axis=0, tiled=True)  128 us
    reduce_scatter x1, waiting for transfers between devices, body(): lax.psum_scatter(grad_groups[0].astype(jnp.float32).astype(jnp.bfloat16),...  103 us
    psum x1, blocking collectives, body(): total = lax.psum(jnp.sum(summed * summed), ('dp', 'shard'))  94.3 us
    all_gather x1, waiting for transfers between devices, fetch_weights(): lax.all_gather(proj, 'dp', axis=0, tiled=True)  68.1 us
    all_gather x1, waiting for transfers between devices, body(): block = lax.all_gather(table, 'dp', axis=0, tiled=True)  42.6 us
    all_gather x1, waiting for transfers between devices, fetch_weights(): lax.all_gather(w_qkv, 'dp', axis=0, tiled=True)  40.7 us
    all_to_all x1, blocking collectives, body(): lax.all_to_all(wanted.reshape(shards, capacity), 'shard', split_axis=0, c...  17 us
    all_to_all x1, waiting for transfers between devices, body(): lax.all_to_all(looked, 'shard', split_axis=0, concat_axis=0, tiled=True)  11.4 us
  transfers between devices with their start and end apart: 6, of which 6 were waited for; matrix products, arithmetic and copies ran while one was open for 2% of the time, Pallas kernels for 0%

commit v1 on v0

v1 whole, which is shorter than its diff:
```python
import math

import jax
import jax.numpy as jnp
from jax import lax
from jax.experimental import pallas as pl
from jax.experimental.pallas import tpu as pltpu
from jax.sharding import PartitionSpec as P

MESH = pl.DeviceIdType.MESH
F32 = jnp.float32
BF16 = jnp.bfloat16
ROWS = 208
PIECES = ((0, 112), (112, 96))
TOTAL_ENTRIES = 106496 * 256


def dot(a, b):
    return lax.dot_general(a, b, (((1,), (0,)), ((), ())), preferred_element_type=F32)


def dot_t(a, b):
    return lax.dot_general(a, b, (((1,), (1,)), ((), ())), preferred_element_type=F32)


def iota(shape, axis):
    return lax.broadcasted_iota(jnp.int32, shape, axis)


def kernel(
    g_ref, master_ref, m1_ref, m2_ref, proj_ref, gain_ref, w_ref, owner_ref, row_ref,
    o_master, o_m1, o_m2, o_q,
    own, buf_a, buf_b1, buf_b2, send_c, buf_c, state, summed_ref,
    tok_mine, tok_all, idx_send, idx_all, onehot, proj_all, part_send, part_all, w_mine, w_all,
    sq1_mine, sq1_all, sq2_mine, sq2_all, rows_send, rows_all, back_send, back_all, gathered,
    local_sem, a_send, a_recv, b1_send, b1_recv, b2_send, b2_recv, c_send, c_recv,
    dp_send, dp_recv, sh_send, sh_recv, z_send, z_recv, y_send, y_recv,
):
    d = lax.axis_index("dp")
    s = lax.axis_index("shard")
    core, x, zh = lax.rem(d, 2), lax.rem(d // 2, 4), d // 8
    y, z = s // 4, lax.rem(s, 4)

    def dp_peer(i):
        kz, kx, kc = i // 8, lax.rem(i // 2, 4), lax.rem(i, 2)
        return lax.rem(zh + kz, 2) * 8 + lax.rem(x + kx, 4) * 2 + lax.rem(core + kc, 2)

    def sh_peer(i):
        return lax.rem(y + i // 4, 8) * 4 + lax.rem(z + lax.rem(i, 4), 4)

    def x_dev(k):
        return (zh * 8 + lax.rem(x + k, 4) * 2 + core, s)

    def y_dev(k):
        return (d, lax.rem(y + k, 8) * 4 + z)

    load_own = pltpu.make_async_copy(g_ref.at[:, :, core], own, local_sem.at[0])
    load_own.start()
    loads = []
    for n, ref in enumerate((master_ref, m1_ref, m2_ref)):
        load = pltpu.make_async_copy(ref, state.at[n], local_sem.at[1 + n])
        load.start()
        loads.append(load)

    barrier = pltpu.get_barrier_semaphore()

    def greet_dp(i, carry):
        pl.semaphore_signal(barrier, inc=1, device_id=(dp_peer(15 - i), s), device_id_type=MESH)
        return carry

    def greet_sh(i, carry):
        pl.semaphore_signal(barrier, inc=1, device_id=(d, sh_peer(31 - i)), device_id_type=MESH)
        return carry

    lax.fori_loop(0, 31, greet_sh, 0)
    lax.fori_loop(0, 15, greet_dp, 0)
    pl.semaphore_wait(barrier, 46)

    finish = []

    def remote(src, dst, send_sem, recv_sem, device):
        copy = pltpu.make_async_remote_copy(
            src_ref=src, dst_ref=dst, send_sem=send_sem, recv_sem=recv_sem,
            device_id=device, device_id_type=MESH,
        )
        copy.start()
        return copy

    def dp_spread(phase, src_of, dst):
        def step(i, carry):
            peer = dp_peer(15 - i)
            remote(src_of(peer), dst, dp_send.at[phase], dp_recv.at[phase], (peer, s))
            return carry

        lax.fori_loop(0, 15, step, 0)

    def sh_spread(phase, src_of, dst):
        def step(i, carry):
            peer = sh_peer(31 - i)
            remote(src_of(peer), dst, sh_send.at[phase], sh_recv.at[phase], (d, peer))
            return carry

        lax.fori_loop(0, 31, step, 0)

    def wait_bytes(ref, sem):
        pltpu.make_async_copy(ref, ref, sem).wait()

    a_copies = []
    for n, k in enumerate((2, 1, 3, 0)):
        xd = lax.rem(x + k, 4)
        a_copies.append(
            remote(
                g_ref.at[:, xd, 1 - core], buf_a.at[:, xd], a_send.at[n], a_recv.at[n],
                (d + 1 - 2 * core, s),
            )
        )

    tok = owner_ref[...] * 256 + row_ref[...]
    tok_tile = jnp.broadcast_to(tok, (8, 128))
    tok_mine[...] = tok_tile
    tok_all[s] = tok_tile
    sh_spread(0, lambda peer: tok_mine, tok_all.at[s])

    load_own.wait()

    def add_pair(zi, xd):
        own[zi, xd] = (own[zi, xd].astype(F32) + buf_a[zi, xd].astype(F32)).astype(BF16)

    x1, x2, x3 = lax.rem(x + 1, 4), lax.rem(x + 2, 4), lax.rem(x + 3, 4)
    a_copies[0].wait_recv()
    for zi in range(2):
        add_pair(zi, x2)
    b1 = []
    for p, (r0, n) in enumerate(PIECES):
        for zi, k in ((0, 1), (1, 3)):
            b1.append(
                remote(
                    own.at[zi, x2, pl.ds(r0, n)], buf_b1.at[zi, pl.ds(r0, n)],
                    b1_send.at[p, zi], b1_recv.at[p, zi], x_dev(k),
                )
            )
    a_copies[1].wait_recv()
    a_copies[2].wait_recv()
    add_pair(1, x1)
    add_pair(0, x3)
    b2 = {}
    for p, (r0, n) in enumerate(PIECES):
        for zi, xd, k in ((1, x1, 1), (0, x3, 3)):
            b2[p, zi, 0] = remote(
                own.at[zi, xd, pl.ds(r0, n)], buf_b2.at[zi, 0, pl.ds(r0, n)],
                b2_send.at[p, zi, 0], b2_recv.at[p, zi, 0], x_dev(k),
            )
    add_pair(0, x1)
    add_pair(1, x3)

    proj_all[pl.ds(pl.multiple_of(d * 16, 16), 16)] = proj_ref[
        :, pl.ds(pl.multiple_of(d * 256, 256), 256)
    ]
    dp_spread(
        0,
        lambda peer: proj_ref.at[:, pl.ds(pl.multiple_of(peer * 256, 256), 256)],
        proj_all.at[pl.ds(pl.multiple_of(d * 16, 16), 16)],
    )

    for p, (r0, n) in enumerate(PIECES):
        for zi, xd, k in ((0, x1, 1), (1, x3, 3)):
            b1[2 * p + zi].wait_recv()
            own[zi, xd, pl.ds(r0, n)] = (
                own[zi, xd, pl.ds(r0, n)].astype(F32) + buf_b1[zi, pl.ds(r0, n)].astype(F32)
            ).astype(BF16)
            b2[p, zi, 1] = remote(
                own.at[zi, xd, pl.ds(r0, n)], buf_b2.at[zi, 1, pl.ds(r0, n)],
                b2_send.at[p, zi, 1], b2_recv.at[p, zi, 1], x_dev(k),
            )
    a_copies[3].wait_recv()
    for zi in range(2):
        add_pair(zi, x)

    wait_bytes(tok_all.at[pl.ds(0, 31)], sh_recv.at[0])
    tokens = tok_all[:, 0, :]
    member = (tokens // 256) == s
    row_plus = (lax.rem(tokens, 256) + 1).astype(F32)
    before = (iota((128, 128), 0) < iota((128, 128), 1)).astype(F32).astype(BF16)
    rank = dot(member.astype(F32).astype(BF16), before)
    lane = iota((32, 128), 1)
    want = jnp.zeros((32, 128), F32)
    for k in range(8):
        chosen = jnp.where(member & (rank == float(k)), row_plus, 0.0)
        want = want + jnp.where(lane == k, jnp.sum(chosen, axis=1, keepdims=True), 0.0)
    line = iota((256, 32), 0)
    pick = iota((256, 32), 1) == lax.rem(line // 8, 2) * 16 + lax.rem(
        line // 16 + 16 - lax.rem(line, 8), 16
    )
    spread = dot(pick.astype(F32).astype(BF16), want.astype(BF16))
    spread = jnp.where(iota((256, 128), 1) == lax.rem(iota((256, 128), 0), 8), spread, 0.0)
    idx_send[...] = dot(spread.astype(BF16), jnp.ones((128, 128), BF16)).astype(BF16)
    mine16 = pl.ds(pl.multiple_of(d * 16, 16), 16)
    idx_all[mine16] = idx_send[mine16]
    dp_spread(
        1,
        lambda peer: idx_send.at[pl.ds(pl.multiple_of(peer * 16, 16), 16)],
        idx_all.at[mine16],
    )

    wait_bytes(proj_all.at[pl.ds(0, 240)], dp_recv.at[0])
    block = proj_all[...]
    scaled = block.astype(F32) * gain_ref[:, pl.ds(pl.multiple_of(d * 256, 256), 256)]
    high = scaled.astype(BF16)
    low = (scaled - high.astype(F32)).astype(BF16)
    weights = w_ref[...]
    folded = (dot_t(weights, high) + dot_t(weights, low)).astype(BF16)
    gram = dot_t(block, block).astype(BF16)
    for o in range(16):
        if o < 12:
            part_send[o, 0:16] = folded[16 * o : 16 * o + 16]
        else:
            part_send[o, 0:16] = jnp.zeros((16, 256), BF16)
        part_send[o, 16:32] = gram[16 * o : 16 * o + 16]
    part_all[d] = part_send[d]
    dp_spread(2, lambda peer: part_send.at[peer], part_all.at[d])

    c_copies = []
    for p, (r0, n) in enumerate(PIECES):
        for zi in range(2):
            b2[p, zi, 0].wait_recv()
            b2[p, zi, 1].wait_recv()

        def total_of(zi):
            return (
                own[zi, x, pl.ds(r0, n)].astype(F32)
                + buf_b2[zi, 0, pl.ds(r0, n)].astype(F32)
                + buf_b2[zi, 1, pl.ds(r0, n)].astype(F32)
            )

        send_c[pl.ds(r0, n)] = total_of(1 - zh).astype(BF16)
        c_copies.append(
            remote(
                send_c.at[pl.ds(r0, n)], buf_c.at[pl.ds(r0, n)], c_send.at[p], c_recv.at[p],
                (lax.rem(d + 8, 16), s),
            )
        )
        summed_ref[pl.ds(r0, n)] = total_of(zh)

    wait_bytes(part_all.at[pl.ds(0, 15)], dp_recv.at[2])
    whole = part_all[0].astype(F32)
    for o in range(1, 16):
        whole = whole + part_all[o].astype(F32)
    w_mine[...] = whole.astype(BF16)
    w_all[d] = whole.astype(BF16)
    dp_spread(3, lambda peer: w_mine, w_all.at[d])

    wait_bytes(idx_all.at[pl.ds(0, 240)], dp_recv.at[1])
    ids = idx_all[...].astype(F32)
    for half in range(2):
        at = (iota((256, 128), 1) + 1 + 128 * half).astype(F32)
        onehot[:, 128 * half : 128 * half + 128] = jnp.where(ids == at, 1.0, 0.0).astype(BF16)

    squares = jnp.zeros((8, 256), F32)
    for p, (r0, n) in enumerate(PIECES):
        c_copies[p].wait_recv()
        total = summed_ref[pl.ds(r0, n)] + buf_c[pl.ds(r0, n)].astype(F32)
        summed_ref[pl.ds(r0, n)] = total
        squares = squares + jnp.sum((total * total).reshape(n // 8, 8, 256), axis=0)
    tile = squares[:, :128] + squares[:, 128:]
    sq1_mine[...] = tile
    sq1_all[d] = tile
    dp_spread(4, lambda peer: sq1_mine, sq1_all.at[d])

    owner_row = (tok // 256).astype(F32)
    owner_line = jnp.broadcast_to(owner_row, (128, 128))
    owner_col = owner_line.T
    earlier = iota((128, 128), 1) < iota((128, 128), 0)
    slot = jnp.sum(jnp.where((owner_col == owner_line) & earlier, 1.0, 0.0), axis=1, keepdims=True)
    place = owner_col[:, 0:1] * 16.0 + slot
    at = iota((128, 512), 1).astype(F32)
    find_left = jnp.where(at == place, 1.0, 0.0).astype(BF16)
    find_right = jnp.where(at == place + 8.0, 1.0, 0.0).astype(BF16)

    wait_bytes(sq1_all.at[pl.ds(0, 15)], dp_recv.at[4])
    tile = jnp.sum(sq1_all[...], axis=0)
    sq2_mine[...] = tile
    sq2_all[s] = tile
    sh_spread(1, lambda peer: sq2_mine, sq2_all.at[s])

    line, col = iota((512, 256), 0), iota((512, 256), 1)
    to, unit = line // 16, lax.rem(line, 16)
    k = lax.rem(unit, 8)
    match = col == lax.rem(to + k, 16) * 16 + (to // 16) * 8 + k
    pack_left = jnp.where(match & (unit < 8), 1.0, 0.0).astype(BF16)
    pack_right = jnp.where(match & (unit >= 8), 1.0, 0.0).astype(BF16)
    for load in loads:
        load.wait()

    wait_bytes(sq2_all.at[pl.ds(0, 31)], sh_recv.at[1])
    total = jnp.sum(sq2_all[...], axis=0)
    total = jnp.sum(jnp.sum(total, axis=0, keepdims=True), axis=1, keepdims=True)
    clip = jnp.minimum(1.0, 0.2 * math.sqrt(TOTAL_ENTRIES) / (jnp.sqrt(total) + 1e-06))
    grad = clip * summed_ref[...]
    new_m1 = 0.9 * state[1] + 0.1 * grad
    new_m2 = 0.95 * state[2] + 0.05 * grad * grad
    one = new_m1 / (1.0 - 0.9**10)
    two = new_m2 / (1.0 - 0.95**10)
    master = state[0]
    new_master = master - 0.01 * (one / (jnp.sqrt(two) + 1e-08) + 0.1 * master)
    o_m1[...] = new_m1
    o_m2[...] = new_m2
    o_master[...] = new_master

    table = new_master.astype(BF16)
    found = dot(onehot[:, 0:ROWS], table).astype(BF16)
    rows_send[...] = found
    rows_all[mine16] = rows_send[mine16]
    dp_spread(
        5,
        lambda peer: rows_send.at[pl.ds(pl.multiple_of(peer * 16, 16), 16)],
        rows_all.at[mine16],
    )
    wait_bytes(rows_all.at[pl.ds(0, 240)], dp_recv.at[5])
    rows = rows_all[...]
    back_send[...] = (dot(pack_left, rows[:, :128]) + dot(pack_right, rows[:, 128:])).astype(BF16)
    mine_s = pl.ds(pl.multiple_of(s * 16, 16), 16)
    back_all[mine_s] = back_send[mine_s]
    sh_spread(
        2,
        lambda peer: back_send.at[pl.ds(pl.multiple_of(peer * 16, 16), 16)],
        back_all.at[mine_s],
    )
    wait_bytes(w_all.at[pl.ds(0, 15)], dp_recv.at[3])
    gram = w_all[:, 16:32, :].reshape(256, 256)
    folded = w_all[0:12, 0:16, :].reshape(192, 256)
    wait_bytes(back_all.at[pl.ds(0, 496)], sh_recv.at[2])
    back = back_all[...]
    rows = jnp.concatenate([dot(find_left, back), dot(find_right, back)], axis=1)
    mean_sq = jnp.sum(dot(rows.astype(BF16), gram) * rows, axis=1, keepdims=True) / 4096.0
    gathered[s] = (rows * lax.rsqrt(mean_sq + 1e-05)).astype(BF16)

    z_copies = []
    for k in range(1, 4):
        z_copies.append(
            remote(
                gathered.at[s], gathered.at[s], z_send.at[4 - k], z_recv.at[4 - k],
                (d, y * 4 + lax.rem(z + k, 4)),
            )
        )

    def project(at):
        o_q[:, pl.ds(pl.multiple_of(at * 128, 128), 128)] = dot_t(folded, gathered[at]).astype(BF16)

    def block_at(step, way, j):
        back_by = (8 - step) if way == 0 else step
        return lax.rem(y + back_by, 8) * 4 + lax.rem(z + j, 4)

    def ring_copy(step, way, j):
        at = block_at(step, way, j)
        return pltpu.make_async_remote_copy(
            src_ref=gathered.at[at], dst_ref=gathered.at[at],
            send_sem=y_send.at[way, step, j], recv_sem=y_recv.at[way, step, j],
            device_id=y_dev(1 if way == 0 else 7), device_id_type=MESH,
        )

    def arrived(step, way, j):
        at = block_at(step, way, j)
        pltpu.make_async_copy(gathered.at[at], gathered.at[at], y_recv.at[way, step - 1, j]).wait()

    for j in range(4):
        if j:
            at = y * 4 + lax.rem(z + j, 4)
            pltpu.make_async_copy(gathered.at[at], gathered.at[at], z_recv.at[j]).wait()
        ring_copy(0, 0, j).start()
        ring_copy(0, 1, j).start()
        project(block_at(0, 0, j))
    for step in (1, 2):
        for j in range(4):
            for way in range(2):
                arrived(step, way, j)
                ring_copy(step, way, j).start()
                project(block_at(step, way, j))
    for j in range(4):
        for way in range(2):
            arrived(3, way, j)
            if j // 2 == way:
                ring_copy(3, way, j).start()
            project(block_at(3, way, j))
    for j in range(4):
        arrived(4, j // 2, j)
        project(block_at(4, j // 2, j))

    for copy in a_copies + b1 + list(b2.values()) + c_copies + z_copies:
        copy.wait_send()
    for phase, ref in enumerate(
        (proj_all.at[pl.ds(0, 240)], idx_all.at[pl.ds(0, 240)], part_all.at[pl.ds(0, 15)],
         w_all.at[pl.ds(0, 15)], sq1_all.at[pl.ds(0, 15)], rows_all.at[pl.ds(0, 240)])
    ):
        wait_bytes(ref, dp_send.at[phase])
    for phase, ref in enumerate(
        (tok_all.at[pl.ds(0, 31)], sq2_all.at[pl.ds(0, 31)], back_all.at[pl.ds(0, 496)])
    ):
        wait_bytes(ref, sh_send.at[phase])
    for step in range(4):
        for j in range(4):
            for way in range(2):
                if step < 3 or j // 2 == way:
                    ring_copy(step, way, j).wait_send()


def body(grad_groups, master, moment1, moment2, proj, ln_gain, w_qkv, token_owner, token_row):
    vmem = pl.BlockSpec(memory_space=pltpu.VMEM)
    hbm = pl.BlockSpec(memory_space=pl.ANY)
    dma = pltpu.SemaphoreType.DMA
    new_master, new_m1, new_m2, qkv_t = pl.pallas_call(
        kernel,
        out_shape=(
            jax.ShapeDtypeStruct((ROWS, 256), F32),
            jax.ShapeDtypeStruct((ROWS, 256), F32),
            jax.ShapeDtypeStruct((ROWS, 256), F32),
            jax.ShapeDtypeStruct((192, 4096), BF16),
        ),
        in_specs=[hbm] * 4 + [vmem] * 5,
        out_specs=[vmem] * 4,
        scratch_shapes=[
            pltpu.VMEM((2, 4, ROWS, 256), BF16),
            pltpu.VMEM((2, 4, ROWS, 256), BF16),
            pltpu.VMEM((2, ROWS, 256), BF16),
            pltpu.VMEM((2, 2, ROWS, 256), BF16),
            pltpu.VMEM((ROWS, 256), BF16),
            pltpu.VMEM((ROWS, 256), BF16),
            pltpu.VMEM((3, ROWS, 256), F32),
            pltpu.VMEM((ROWS, 256), F32),
            pltpu.VMEM((8, 128), jnp.int32),
            pltpu.VMEM((32, 8, 128), jnp.int32),
            pltpu.VMEM((256, 128), BF16),
            pltpu.VMEM((256, 128), BF16),
            pltpu.VMEM((256, 256), BF16),
            pltpu.VMEM((256, 256), BF16),
            pltpu.VMEM((16, 32, 256), BF16),
            pltpu.VMEM((16, 32, 256), BF16),
            pltpu.VMEM((32, 256), BF16),
            pltpu.VMEM((16, 32, 256), BF16),
            pltpu.VMEM((8, 128), F32),
            pltpu.VMEM((16, 8, 128), F32),
            pltpu.VMEM((8, 128), F32),
            pltpu.VMEM((32, 8, 128), F32),
            pltpu.VMEM((256, 256), BF16),
            pltpu.VMEM((256, 256), BF16),
            pltpu.VMEM((512, 128), BF16),
            pltpu.VMEM((512, 128), BF16),
            pltpu.VMEM((32, 128, 256), BF16),
            dma((4,)),
            dma((4,)), dma((4,)),
            dma((2, 2)), dma((2, 2)),
            dma((2, 2, 2)), dma((2, 2, 2)),
            dma((2,)), dma((2,)),
            dma((6,)), dma((6,)),
            dma((3,)), dma((3,)),
            dma((4,)), dma((4,)),
            dma((2, 4, 4)), dma((2, 4, 4)),
        ],
        compiler_params=pltpu.CompilerParams(
            collective_id=0, has_side_effects=True, vmem_limit_bytes=40 << 20
        ),
        name="step",
    )(
        grad_groups.reshape(2, 4, 2, ROWS, 256),
        master,
        moment1,
        moment2,
        proj,
        ln_gain.reshape(1, 4096),
        w_qkv.T,
        token_owner.reshape(1, 128),
        token_row.reshape(1, 128),
    )
    return new_master, new_m1, new_m2, qkv_t.T


def solution(mesh):
    placed = (
        P("dp", "shard", None),
        P(("shard", "dp"), None),
        P(("shard", "dp"), None),
        P(("shard", "dp"), None),
        P("dp", None),
        P(),
        P("dp", "shard"),
        P(("dp", "shard"), None),
        P(("dp", "shard")),
    )
    return jax.shard_map(
        body,
        mesh=mesh,
        in_specs=placed,
        out_specs=(
            P(("shard", "dp"), None),
            P(("shard", "dp"), None),
            P(("shard", "dp"), None),
            P("dp", "shard"),
        ),
        check_vma=False,
    )
```

time: 554 us -> 112 us (0.20)
  the two profiles are of different devices: /device:TPU:6 before, /device:TPU:120 now
where the time goes in v1:
time: 112 us
  Pallas kernels  99.8 us (89%)
  local copies, waits for them, and re-layouts  11.3 us (10%)
    pallas_call x1, Pallas kernels, body(): pl.pallas_call(kernel, out_shape=(jax.ShapeDtypeStruct((ROWS, 256), F32),...  99.8 us
    unnamed x22, local copies, waits for them, and re-layouts  11.3 us

profile of v1, /device:TPU:120, one launch (start us, length us, event | category | flops | bytes accessed | tf_op | source)
XLA Modules:
  0.0 111.7 jit_solution(263577808470760196)
XLA Ops:
  0.6 0.0 copy-start
  0.6 1.4 %copy-done = bf16[1,3328,256]{2,1,0:T(8,128)(2,1)S(1)} copy-done((bf16[1,3328,256]{2,1,0:T(8,128)(2,1)S(1)}, bf16[1,3328,256]{2,1,0:T(8,128)(2,1)}, u32[]{:S(2)}) %copy-start) | copy-done | bytes 1703960
  2.1 0.0 copy-start.1
  2.1 0.9 copy-done.1
  3.0 0.0 copy-start.2
  3.0 0.9 copy-done.2
  4.0 0.0 copy-start.3
  4.0 0.9 copy-done.3
  4.9 0.0 copy-start.4
  4.9 0.9 copy-done.4
  5.8 0.0 copy-start.5
  5.8 0.9 copy-done.5
  6.7 0.0 copy-start.6
  6.7 0.7 copy-done.6
  7.4 0.0 copy-start.7
  7.4 0.7 copy-done.7
  8.1 0.0 copy-start.8
  8.1 0.7 copy-done.8
  8.7 99.8 %step.1 = (f32[208,256]{1,0:T(8,128)S(1)}, f32[208,256]{1,0:T(8,128)S(1)}, f32[208,256]{1,0:T(8,128)S(1)}, bf16[192,4096]{1,0:T(8,128)(2,1)S(1)}) custom-call(bf16[2,4,2,208,256]{4,3,2,1,0:T(8,128)(2,1)S(1)} %bitcast.6, f32[208,256]{1,0:T(8,128)S(1)} %copy-done.1, f32[208,256]{1,0:T(8,128)S(1)} %copy-done.2, f32[208,256]{1,0:T(8,128)S(1)} %copy-done.3, ...), custom_call_target="tpu_custom_call" | custom-call | tf_op jit(solution)/shard_map/step/pallas_call | solution.py:410
  108.5 0.7 copy.17
  109.2 0.7 copy.18
  109.9 0.7 copy.19
  110.6 1.1 %copy.20 = bf16[4096,192]{0,1:T(8,128)(2,1)} copy(bf16[4096,192]{0,1:T(8,128)(2,1)S(1)} %bitcast.7) | data formatting | bytes 3145728
Async XLA Ops:
  0.6 1.5 %copy-start = (bf16[1,3328,256]{2,1,0:T(8,128)(2,1)S(1)}, bf16[1,3328,256]{2,1,0:T(8,128)(2,1)}, u32[]{:S(2)}) copy-start(bf16[1,3328,256]{2,1,0:T(8,128)(2,1)} %param.9) | copy-start | bytes 5111812
  2.1 0.9 copy-start.1
  3.0 0.9 copy-start.2
  4.0 0.9 copy-start.3
  4.9 0.9 copy-start.4
  5.8 0.9 copy-start.5
  6.7 0.7 copy-start.6
  7.4 0.7 copy-start.7
  8.1 0.7 copy-start.8

commit v2 on v1

v2 whole, which is shorter than its diff:
```python
import math

import jax
import jax.numpy as jnp
from jax import lax
from jax.experimental import pallas as pl
from jax.experimental.pallas import tpu as pltpu
from jax.sharding import PartitionSpec as P

MESH = pl.DeviceIdType.MESH
F32 = jnp.float32
BF16 = jnp.bfloat16
ROWS = 208
FIRST = 96
PIECES = ((0, 112), (112, 96))
TOTAL_ENTRIES = 106496 * 256


def dot(a, b):
    return lax.dot_general(a, b, (((1,), (0,)), ((), ())), preferred_element_type=F32)


def dot_t(a, b):
    return lax.dot_general(a, b, (((1,), (1,)), ((), ())), preferred_element_type=F32)


def iota(shape, axis):
    return lax.broadcasted_iota(jnp.int32, shape, axis)


def kernel(
    g_ref, master_ref, m1_ref, m2_ref, proj_hbm, gain_hbm, w_hbm, owner_hbm, row_hbm,
    o_master, o_m1, o_m2, o_q,
    proj_ref, gain_ref, w_ref, owner_ref, row_ref,
    own, buf_a, buf_b1, buf_b2, send_c, buf_c, state, summed_ref,
    tok_mine, tok_all, idx_send, idx_all, onehot, proj_all, part_send, part_all, w_mine, w_all,
    sq1_mine, sq1_all, sq2_mine, sq2_all, rows_send, rows_all, back_send, back_all, gathered, qkv,
    local_sem, out_sem, a_send, a_recv, b1_send, b1_recv, b2_send, b2_recv, c_send, c_recv,
    dp_send, dp_recv, sh_send, sh_recv, z_send, z_recv, y_send, y_recv, yl_send, yl_recv, zl_send, zl_recv,
):
    d = lax.axis_index("dp")
    s = lax.axis_index("shard")
    core, x, zh = lax.rem(d, 2), lax.rem(d // 2, 4), d // 8
    y, z = s // 4, lax.rem(s, 4)

    def dp_peer(i):
        kz, kx, kc = i // 8, lax.rem(i // 2, 4), lax.rem(i, 2)
        return lax.rem(zh + kz, 2) * 8 + lax.rem(x + kx, 4) * 2 + lax.rem(core + kc, 2)

    def sh_peer(i):
        return lax.rem(y + i // 4, 8) * 4 + lax.rem(z + lax.rem(i, 4), 4)

    def x_dev(k):
        return (zh * 8 + lax.rem(x + k, 4) * 2 + core, s)

    def y_dev(k):
        return (d, lax.rem(y + k, 8) * 4 + z)

    loads = []
    for n, (src, dst) in enumerate(
        (
            (owner_hbm, owner_ref), (row_hbm, row_ref), (g_ref.at[:, :, core], own),
            (proj_hbm, proj_ref), (w_hbm, w_ref), (gain_hbm, gain_ref),
            (master_ref, state.at[0]), (m1_ref, state.at[1]), (m2_ref, state.at[2]),
        )
    ):
        load = pltpu.make_async_copy(src, dst, local_sem.at[n])
        load.start()
        loads.append(load)

    barrier = pltpu.get_barrier_semaphore()

    def greet_dp(i, carry):
        pl.semaphore_signal(barrier, inc=1, device_id=(dp_peer(1 + i), s), device_id_type=MESH)
        return carry

    def greet_sh(i, carry):
        pl.semaphore_signal(barrier, inc=1, device_id=(d, sh_peer(1 + i)), device_id_type=MESH)
        return carry

    lax.fori_loop(0, 15, greet_dp, 0)
    lax.fori_loop(0, 31, greet_sh, 0)
    pl.semaphore_wait(barrier, 46)

    sent = []

    def copy_to(src, dst, send_sem, recv_sem, device):
        return pltpu.make_async_remote_copy(
            src_ref=src, dst_ref=dst, send_sem=send_sem, recv_sem=recv_sem,
            device_id=device, device_id_type=MESH,
        )

    def remote(src, dst, send_sem, recv_sem, device):
        copy = copy_to(src, dst, send_sem, recv_sem, device)
        copy.start()
        sent.append(copy.wait_send)
        return copy

    def dp_spread(phase, batch, src_of, dst):
        def step(i, carry):
            peer = dp_peer(15 - i)
            copy_to(src_of(peer), dst, dp_send.at[phase], dp_recv.at[phase], (peer, s)).start()
            return carry

        lax.fori_loop(0, 15, step, 0)
        sent.append(lambda: wait_bytes(batch, dp_send.at[phase]))
        return lambda: wait_bytes(batch, dp_recv.at[phase])

    def sh_spread(phase, batch, src_of, dst):
        def step(i, carry):
            peer = sh_peer(31 - i)
            copy_to(src_of(peer), dst, sh_send.at[phase], sh_recv.at[phase], (d, peer)).start()
            return carry

        lax.fori_loop(0, 31, step, 0)
        sent.append(lambda: wait_bytes(batch, sh_send.at[phase]))
        return lambda: wait_bytes(batch, sh_recv.at[phase])

    def wait_bytes(ref, sem):
        pltpu.make_async_copy(ref, ref, sem).wait()

    a_copies = []
    for n, k in enumerate((2, 1, 3, 0)):
        xd = lax.rem(x + k, 4)
        a_copies.append(
            remote(
                g_ref.at[:, xd, 1 - core], buf_a.at[:, xd], a_send.at[n], a_recv.at[n],
                (d + 1 - 2 * core, s),
            )
        )

    loads[2].wait()

    def add_pair(zi, xd):
        own[zi, xd] = (own[zi, xd].astype(F32) + buf_a[zi, xd].astype(F32)).astype(BF16)

    x1, x2, x3 = lax.rem(x + 1, 4), lax.rem(x + 2, 4), lax.rem(x + 3, 4)
    a_copies[0].wait_recv()
    for zi in range(2):
        add_pair(zi, x2)
    b1 = []
    for p, (r0, n) in enumerate(PIECES):
        for zi, k in ((0, 1), (1, 3)):
            b1.append(
                remote(
                    own.at[zi, x2, pl.ds(r0, n)], buf_b1.at[zi, pl.ds(r0, n)],
                    b1_send.at[p, zi], b1_recv.at[p, zi], x_dev(k),
                )
            )
    loads[0].wait()
    loads[1].wait()
    tok = owner_ref[...] * 256 + row_ref[...]
    tok_tile = jnp.broadcast_to(tok, (8, 128))
    tok_mine[...] = tok_tile
    tok_all[s] = tok_tile
    tokens_in = sh_spread(0, tok_all.at[pl.ds(0, 31)], lambda peer: tok_mine, tok_all.at[s])

    a_copies[1].wait_recv()
    a_copies[2].wait_recv()
    add_pair(1, x1)
    add_pair(0, x3)
    b2 = {}
    for p, (r0, n) in enumerate(PIECES):
        for zi, xd, k in ((1, x1, 1), (0, x3, 3)):
            b2[p, zi, 0] = remote(
                own.at[zi, xd, pl.ds(r0, n)], buf_b2.at[zi, 0, pl.ds(r0, n)],
                b2_send.at[p, zi, 0], b2_recv.at[p, zi, 0], x_dev(k),
            )
    add_pair(0, x1)
    add_pair(1, x3)

    for p, (r0, n) in enumerate(PIECES):
        for zi, xd, k in ((0, x1, 1), (1, x3, 3)):
            b1[2 * p + zi].wait_recv()
            own[zi, xd, pl.ds(r0, n)] = (
                own[zi, xd, pl.ds(r0, n)].astype(F32) + buf_b1[zi, pl.ds(r0, n)].astype(F32)
            ).astype(BF16)
            b2[p, zi, 1] = remote(
                own.at[zi, xd, pl.ds(r0, n)], buf_b2.at[zi, 1, pl.ds(r0, n)],
                b2_send.at[p, zi, 1], b2_recv.at[p, zi, 1], x_dev(k),
            )
    loads[3].wait()
    proj_all[pl.ds(pl.multiple_of(d * 16, 16), 16)] = proj_ref[
        :, pl.ds(pl.multiple_of(d * 256, 256), 256)
    ]
    proj_in = dp_spread(
        0,
        proj_all.at[pl.ds(0, 240)],
        lambda peer: proj_ref.at[:, pl.ds(pl.multiple_of(peer * 256, 256), 256)],
        proj_all.at[pl.ds(pl.multiple_of(d * 16, 16), 16)],
    )

    a_copies[3].wait_recv()
    for zi in range(2):
        add_pair(zi, x)

    tokens_in()
    tokens = tok_all[:, 0, :]
    member = (tokens >> 8) == s
    row_plus = ((tokens & 255) + 1).astype(F32)
    before = (iota((128, 128), 0) < iota((128, 128), 1)).astype(F32).astype(BF16)
    rank = dot(member.astype(F32).astype(BF16), before)
    lane = iota((32, 128), 1)
    want = jnp.zeros((32, 128), F32)
    for k in range(8):
        chosen = jnp.where(member & (rank == float(k)), row_plus, 0.0)
        want = want + jnp.where(lane == k, jnp.sum(chosen, axis=1, keepdims=True), 0.0)
    line = iota((256, 32), 0)
    pick = iota((256, 32), 1) == ((line >> 3) & 1) * 16 + (((line >> 4) - (line & 7)) & 15)
    spread = dot(pick.astype(F32).astype(BF16), want.astype(BF16))
    spread = jnp.where(iota((256, 128), 1) == (iota((256, 128), 0) & 7), spread, 0.0)
    idx_send[...] = dot(spread.astype(BF16), jnp.ones((128, 128), BF16)).astype(BF16)
    mine16 = pl.ds(pl.multiple_of(d * 16, 16), 16)
    idx_all[mine16] = idx_send[mine16]
    idx_in = dp_spread(
        1,
        idx_all.at[pl.ds(0, 240)],
        lambda peer: idx_send.at[pl.ds(pl.multiple_of(peer * 16, 16), 16)],
        idx_all.at[mine16],
    )

    c_copies = []
    for p, (r0, n) in enumerate(PIECES):
        for zi in range(2):
            b2[p, zi, 0].wait_recv()
            b2[p, zi, 1].wait_recv()

        def total_of(zi):
            return (
                own[zi, x, pl.ds(r0, n)].astype(F32)
                + buf_b2[zi, 0, pl.ds(r0, n)].astype(F32)
                + buf_b2[zi, 1, pl.ds(r0, n)].astype(F32)
            )

        send_c[pl.ds(r0, n)] = total_of(1 - zh).astype(BF16)
        c_copies.append(
            remote(
                send_c.at[pl.ds(r0, n)], buf_c.at[pl.ds(r0, n)], c_send.at[p], c_recv.at[p],
                (lax.rem(d + 8, 16), s),
            )
        )
        summed_ref[pl.ds(r0, n)] = total_of(zh)

    proj_in()
    loads[4].wait()
    loads[5].wait()
    block = proj_all[...]
    scaled = block.astype(F32) * gain_ref[:, pl.ds(pl.multiple_of(d * 256, 256), 256)]
    high = scaled.astype(BF16)
    low = (scaled - high.astype(F32)).astype(BF16)
    weights = w_ref[...]
    folded = (dot_t(weights, high) + dot_t(weights, low)).astype(BF16)
    gram = dot_t(block, block).astype(BF16)
    for o in range(16):
        if o < 12:
            part_send[o, 0:16] = folded[16 * o : 16 * o + 16]
        else:
            part_send[o, 0:16] = jnp.zeros((16, 256), BF16)
        part_send[o, 16:32] = gram[16 * o : 16 * o + 16]
    part_all[d] = part_send[d]
    idx_in()
    ids = idx_all[...].astype(F32)
    for half in range(2):
        at = (iota((256, 128), 1) + 1 + 128 * half).astype(F32)
        onehot[:, 128 * half : 128 * half + 128] = jnp.where(ids == at, 1.0, 0.0).astype(BF16)

    squares = jnp.zeros((8, 256), F32)
    for p, (r0, n) in enumerate(PIECES):
        c_copies[p].wait_recv()
        total = summed_ref[pl.ds(r0, n)] + buf_c[pl.ds(r0, n)].astype(F32)
        summed_ref[pl.ds(r0, n)] = total
        squares = squares + jnp.sum((total * total).reshape(n // 8, 8, 256), axis=0)
    tile = squares[:, :128] + squares[:, 128:]
    sq1_mine[...] = tile
    sq1_all[d] = tile
    sq1_in = dp_spread(4, sq1_all.at[pl.ds(0, 15)], lambda peer: sq1_mine, sq1_all.at[d])

    part_in = dp_spread(2, part_all.at[pl.ds(0, 15)], lambda peer: part_send.at[peer], part_all.at[d])

    owner_row = (tok >> 8).astype(F32)
    owner_line = jnp.broadcast_to(owner_row, (128, 128))
    owner_col = owner_line.T
    earlier = iota((128, 128), 1) < iota((128, 128), 0)
    slot = jnp.sum(jnp.where((owner_col == owner_line) & earlier, 1.0, 0.0), axis=1, keepdims=True)
    place = owner_col[:, 0:1] * 16.0 + slot
    at = iota((128, 512), 1).astype(F32)
    find_left = jnp.where(at == place, 1.0, 0.0).astype(BF16)
    find_right = jnp.where(at == place + 8.0, 1.0, 0.0).astype(BF16)

    sq1_in()
    tile = jnp.sum(sq1_all[...], axis=0)
    sq2_mine[...] = tile
    sq2_all[s] = tile
    sq2_in = sh_spread(1, sq2_all.at[pl.ds(0, 31)], lambda peer: sq2_mine, sq2_all.at[s])

    line, col = iota((512, 256), 0), iota((512, 256), 1)
    to, unit = line >> 4, line & 15
    k = unit & 7
    match = col == ((to + k) & 15) * 16 + (to >> 4) * 8 + k
    pack_left = jnp.where(match & (unit < 8), 1.0, 0.0).astype(BF16)
    pack_right = jnp.where(match & (unit >= 8), 1.0, 0.0).astype(BF16)
    part_in()
    whole = part_all[0].astype(F32)
    for o in range(1, 16):
        whole = whole + part_all[o].astype(F32)
    w_mine[...] = whole.astype(BF16)
    w_all[d] = whole.astype(BF16)
    weights_in = dp_spread(3, w_all.at[pl.ds(0, 15)], lambda peer: w_mine, w_all.at[d])

    for load in loads[6:]:
        load.wait()

    sq2_in()
    total = jnp.sum(sq2_all[...], axis=0)
    total = jnp.sum(jnp.sum(total, axis=0, keepdims=True), axis=1, keepdims=True)
    clip = jnp.minimum(1.0, 0.2 * math.sqrt(TOTAL_ENTRIES) / (jnp.sqrt(total) + 1e-06))
    grad = clip * summed_ref[...]
    new_m1 = 0.9 * state[1] + 0.1 * grad
    new_m2 = 0.95 * state[2] + 0.05 * grad * grad
    one = new_m1 / (1.0 - 0.9**10)
    two = new_m2 / (1.0 - 0.95**10)
    master = state[0]
    new_master = master - 0.01 * (one / (jnp.sqrt(two) + 1e-08) + 0.1 * master)
    table = new_master.astype(BF16)
    found = dot(onehot[:, 0:ROWS], table).astype(BF16)
    rows_send[...] = found
    rows_all[mine16] = rows_send[mine16]
    rows_in = dp_spread(
        5,
        rows_all.at[pl.ds(0, 240)],
        lambda peer: rows_send.at[pl.ds(pl.multiple_of(peer * 16, 16), 16)],
        rows_all.at[mine16],
    )
    state[0] = new_master
    state[1] = new_m1
    state[2] = new_m2
    for n, ref in enumerate((o_master, o_m1, o_m2)):
        store = pltpu.make_async_copy(state.at[n], ref, out_sem.at[n])
        store.start()
        sent.append(store.wait)
    rows_in()
    rows = rows_all[...]
    back_send[...] = (dot(pack_left, rows[:, :128]) + dot(pack_right, rows[:, 128:])).astype(BF16)
    mine_s = pl.ds(pl.multiple_of(s * 16, 16), 16)
    back_all[mine_s] = back_send[mine_s]
    back_in = sh_spread(
        2,
        back_all.at[pl.ds(0, 496)],
        lambda peer: back_send.at[pl.ds(pl.multiple_of(peer * 16, 16), 16)],
        back_all.at[mine_s],
    )
    weights_in()
    gram = w_all[:, 16:32, :].reshape(256, 256)
    folded = w_all[0:12, 0:16, :].reshape(192, 256)
    back_in()
    back = back_all[...]
    rows = jnp.concatenate([dot(find_left, back), dot(find_right, back)], axis=1)
    mean_sq = jnp.sum(dot(rows.astype(BF16), gram) * rows, axis=1, keepdims=True) / 4096.0
    gathered[s] = (rows * lax.rsqrt(mean_sq + 1e-05)).astype(BF16)

    first, last = pl.ds(0, FIRST), pl.ds(FIRST, 128 - FIRST)

    def block_at(step, way, j):
        back_by = (8 - step) if way == 0 else step
        return lax.rem(y + back_by, 8) * 4 + lax.rem(z + j, 4)

    def ring_to(way):
        return y_dev(1 if way == 0 else 7)

    def first_on(step, way, j):
        part = gathered.at[block_at(step, way, j), first]
        remote(part, part, y_send.at[way, step, j], y_recv.at[way, step, j], ring_to(way))

    def first_in(step, way, j):
        part = gathered.at[block_at(step, way, j), first]
        wait_bytes(part, y_recv.at[way, step - 1, j])

    def last_rows(step, way):
        if step < 3:
            return last
        half = (128 - FIRST) // 2
        return pl.ds(FIRST + way * half, half)

    def last_on(step, way):
        part = gathered.at[block_at(step, way, 0), last_rows(step, way)]
        remote(part, part, yl_send.at[way, step], yl_recv.at[way, step], ring_to(way))

    def last_in(step, way):
        part = gathered.at[block_at(step, way, 0), last_rows(step - 1, way)]
        wait_bytes(part, yl_recv.at[way, step - 1])

    def last_along_z(step, way):
        part = gathered.at[block_at(step, way, 0), last]
        for k in (2, 1, 3):
            remote(
                part, part, zl_send.at[way, step - 1, 4 - k], zl_recv.at[way, step - 1, 4 - k],
                (d, y * 4 + lax.rem(z + k, 4)),
            )

    def project(step, way, j):
        at = block_at(step, way, j)
        if step and j:
            wait_bytes(gathered.at[at, last], zl_recv.at[way, step - 1, j])
        columns = pl.ds(pl.multiple_of(at * 128, 128), 128)
        qkv[:, columns] = dot_t(folded, gathered[at]).astype(BF16)
        pltpu.make_async_copy(qkv.at[:, columns], o_q.at[:, columns], out_sem.at[3]).start()

    for way in range(2):
        last_on(0, way)
    for k in (2, 1, 3):
        remote(
            gathered.at[s], gathered.at[s], z_send.at[4 - k], z_recv.at[4 - k],
            (d, y * 4 + lax.rem(z + k, 4)),
        )
    for j in range(4):
        if j:
            wait_bytes(gathered.at[block_at(0, 0, j)], z_recv.at[j])
        for way in range(2):
            first_on(0, way, j)
        project(0, 0, j)
    for step in (1, 2, 3):
        for way in range(2):
            last_in(step, way)
            last_on(step, way)
            last_along_z(step, way)
        for j in range(4):
            for way in range(2):
                first_in(step, way, j)
                if step < 3 or j // 2 == way:
                    first_on(step, way, j)
        if step > 1:
            for j in range(4):
                for way in range(2):
                    project(step - 1, way, j)
    for way in range(2):
        last_in(4, way)
    last_along_z(4, 0)
    for j in range(4):
        for way in range(2):
            project(3, way, j)
    for j in range(4):
        first_in(4, j // 2, j)
        project(4, 0, j)

    wait_bytes(qkv, out_sem.at[3])
    for wait in sent:
        wait()


def store_kernel(*refs):
    sources, targets, held, sem = refs[:4], refs[4:8], refs[8:12], refs[12]
    parts = [(n, slice(None)) for n in range(3)] + [(3, pl.ds(1024 * c, 1024)) for c in range(4)]
    loads = [
        pltpu.make_async_copy(sources[n].at[:, at], held[n].at[:, at], sem.at[0, i])
        for i, (n, at) in enumerate(parts)
    ]
    stores = [
        pltpu.make_async_copy(held[n].at[:, at], targets[n].at[:, at], sem.at[1, i])
        for i, (n, at) in enumerate(parts)
    ]
    for load in loads:
        load.start()
    for load, store in zip(loads, stores):
        load.wait()
        store.start()
    for store in stores:
        store.wait()


def body(grad_groups, master, moment1, moment2, proj, ln_gain, w_qkv, token_owner, token_row):
    hbm = pl.BlockSpec(memory_space=pltpu.HBM)
    dma = pltpu.SemaphoreType.DMA
    results = pl.pallas_call(
        kernel,
        out_shape=(
            jax.ShapeDtypeStruct((ROWS, 256), F32),
            jax.ShapeDtypeStruct((ROWS, 256), F32),
            jax.ShapeDtypeStruct((ROWS, 256), F32),
            jax.ShapeDtypeStruct((192, 4096), BF16),
        ),
        in_specs=[hbm] * 9,
        out_specs=[hbm] * 4,
        scratch_shapes=[
            pltpu.VMEM((16, 4096), BF16),
            pltpu.VMEM((1, 4096), F32),
            pltpu.VMEM((192, 256), BF16),
            pltpu.VMEM((1, 128), jnp.int32),
            pltpu.VMEM((1, 128), jnp.int32),
            pltpu.VMEM((2, 4, ROWS, 256), BF16),
            pltpu.VMEM((2, 4, ROWS, 256), BF16),
            pltpu.VMEM((2, ROWS, 256), BF16),
            pltpu.VMEM((2, 2, ROWS, 256), BF16),
            pltpu.VMEM((ROWS, 256), BF16),
            pltpu.VMEM((ROWS, 256), BF16),
            pltpu.VMEM((3, ROWS, 256), F32),
            pltpu.VMEM((ROWS, 256), F32),
            pltpu.VMEM((8, 128), jnp.int32),
            pltpu.VMEM((32, 8, 128), jnp.int32),
            pltpu.VMEM((256, 128), BF16),
            pltpu.VMEM((256, 128), BF16),
            pltpu.VMEM((256, 256), BF16),
            pltpu.VMEM((256, 256), BF16),
            pltpu.VMEM((16, 32, 256), BF16),
            pltpu.VMEM((16, 32, 256), BF16),
            pltpu.VMEM((32, 256), BF16),
            pltpu.VMEM((16, 32, 256), BF16),
            pltpu.VMEM((8, 128), F32),
            pltpu.VMEM((16, 8, 128), F32),
            pltpu.VMEM((8, 128), F32),
            pltpu.VMEM((32, 8, 128), F32),
            pltpu.VMEM((256, 256), BF16),
            pltpu.VMEM((256, 256), BF16),
            pltpu.VMEM((512, 128), BF16),
            pltpu.VMEM((512, 128), BF16),
            pltpu.VMEM((32, 128, 256), BF16),
            pltpu.VMEM((192, 4096), BF16),
            dma((9,)),
            dma((4,)),
            dma((4,)), dma((4,)),
            dma((2, 2)), dma((2, 2)),
            dma((2, 2, 2)), dma((2, 2, 2)),
            dma((2,)), dma((2,)),
            dma((6,)), dma((6,)),
            dma((3,)), dma((3,)),
            dma((4,)), dma((4,)),
            dma((2, 4, 4)), dma((2, 4, 4)),
            dma((2, 4)), dma((2, 4)),
            dma((2, 4, 4)), dma((2, 4, 4)),
        ],
        compiler_params=pltpu.CompilerParams(
            collective_id=0, has_side_effects=True, vmem_limit_bytes=56 << 20
        ),
        name="step",
    )(
        grad_groups.reshape(2, 4, 2, ROWS, 256),
        master,
        moment1,
        moment2,
        proj,
        ln_gain.reshape(1, 4096),
        w_qkv.T,
        token_owner.reshape(1, 128),
        token_row.reshape(1, 128),
    )
    new_master, new_m1, new_m2, qkv_t = pl.pallas_call(
        store_kernel,
        out_shape=tuple(jax.ShapeDtypeStruct(a.shape, a.dtype) for a in results),
        in_specs=[pl.BlockSpec(memory_space=pl.ANY)] * 4,
        out_specs=[hbm] * 4,
        scratch_shapes=[pltpu.VMEM(a.shape, a.dtype) for a in results] + [dma((2, 7))],
        name="store",
    )(*results)
    return new_master, new_m1, new_m2, qkv_t.T


def solution(mesh):
    placed = (
        P("dp", "shard", None),
        P(("shard", "dp"), None),
        P(("shard", "dp"), None),
        P(("shard", "dp"), None),
        P("dp", None),
        P(),
        P("dp", "shard"),
        P(("dp", "shard"), None),
        P(("dp", "shard")),
    )
    return jax.shard_map(
        body,
        mesh=mesh,
        in_specs=placed,
        out_specs=(
            P(("shard", "dp"), None),
            P(("shard", "dp"), None),
            P(("shard", "dp"), None),
            P("dp", "shard"),
        ),
        check_vma=False,
    )
```

time: 112 us -> 101 us (0.902)
  the two profiles are of different devices: /device:TPU:120 before, /device:TPU:6 now
where the time goes in v2:
time: 101 us; the launch traced here: 100 us
  Pallas kernels  99.8 us (99%)
    pallas_call x1, Pallas kernels, body(): pl.pallas_call(kernel, out_shape=(jax.ShapeDtypeStruct((ROWS, 256), F32),...  97.3 us
    pallas_call x1, Pallas kernels, body(): pl.pallas_call(store_kernel, out_shape=tuple((jax.ShapeDtypeStruct(a.shap...  2.57 us

profile of v2, /device:TPU:6, one launch (start us, length us, event | category | flops | bytes accessed | tf_op | source)
XLA Modules:
  0.0 100.5 jit_solution(784528819966495592)
XLA Ops:
  0.6 97.3 %step.1 = (f32[208,256]{1,0:T(8,128)}, f32[208,256]{1,0:T(8,128)}, f32[208,256]{1,0:T(8,128)}, bf16[192,4096]{1,0:T(8,128)(2,1)}) custom-call(bf16[2,4,2,208,256]{4,3,2,1,0:T(8,128)(2,1)} %bitcast.6, f32[208,256]{1,0:T(8,128)} %master_ref.1, f32[208,256]{1,0:T(8,128)} %m1_ref.1, f32[208,256]{1,0:T(8,128)} %m2_ref.1, bf16[16,4096]{1,0:T(8,128)(2,1)} %proj_hbm.1, ...), custom_call_target="tpu_custom_call" | custom-call | tf_op jit(solution)/shard_map/step/pallas_call | solution.py:473
  97.9 2.6 %store.1 = (f32[208,256]{1,0:T(8,128)}, f32[208,256]{1,0:T(8,128)}, f32[208,256]{1,0:T(8,128)}, bf16[192,4096]{1,0:T(8,128)(2,1)}) custom-call(f32[208,256]{1,0:T(8,128)} %get-tuple-element.12.refs_0_, f32[208,256]{1,0:T(8,128)} %get-tuple-element.13.refs_1_, f32[208,256]{1,0:T(8,128)} %get-tuple-element.14.refs_2_, bf16[192,4096]{1,0:T(8,128)(2,1)} %get-tuple-element.15.refs_3_), custom_call_target="tpu_custom_call" | custom-call | tf_op jit(solution)/shard_map/store/pallas_call | solution.py:545

commit v3 on v2

--- a/solution.py
+++ b/solution.py
@@ -33,10 +33,10 @@
     o_master, o_m1, o_m2, o_q,
     proj_ref, gain_ref, w_ref, owner_ref, row_ref,
     own, buf_a, buf_b1, buf_b2, send_c, buf_c, state, summed_ref,
-    tok_mine, tok_all, idx_send, idx_all, onehot, proj_all, part_send, part_all, w_mine, w_all,
-    sq1_mine, sq1_all, sq2_mine, sq2_all, rows_send, rows_all, back_send, back_all, gathered, qkv,
+    tok_mine, tok_all, idx_send, idx_all, onehot, proj_all, part_send, part_a, part_sum, part_b, w_pair, w_all,
+    sq_mine, sq_all, rows_send, rows_all, back_send, back_all, gathered, qkv,
     local_sem, out_sem, a_send, a_recv, b1_send, b1_recv, b2_send, b2_recv, c_send, c_recv,
-    dp_send, dp_recv, sh_send, sh_recv, z_send, z_recv, y_send, y_recv, yl_send, yl_recv, zl_send, zl_recv,
+    dp_send, dp_recv, sh_send, sh_recv, few_send, few_recv, w_send, w_recv, z_send, z_recv, y_send, y_recv, yl_send, yl_recv, zl_send, zl_recv,
 ):
     d = lax.axis_index("dp")
     s = lax.axis_index("shard")
@@ -49,6 +49,10 @@
 
     def sh_peer(i):
         return lax.rem(y + i // 4, 8) * 4 + lax.rem(z + lax.rem(i, 4), 4)
+
+    def far_dev(i):
+        at = lax.rem(zh * 4 + z + i, 8)
+        return ((at // 4) * 8 + lax.rem(d, 8), y * 4 + lax.rem(at, 4))
 
     def x_dev(k):
         return (zh * 8 + lax.rem(x + k, 4) * 2 + core, s)
@@ -78,9 +82,15 @@
         pl.semaphore_signal(barrier, inc=1, device_id=(d, sh_peer(1 + i)), device_id_type=MESH)
         return carry
 
+    for i in (1, 2, 3, 5, 6, 7):
+
+        @pl.when(lax.rem(z + i, 8) >= 4)
+        def _():
+            pl.semaphore_signal(barrier, inc=1, device_id=far_dev(i), device_id_type=MESH)
+
     lax.fori_loop(0, 15, greet_dp, 0)
     lax.fori_loop(0, 31, greet_sh, 0)
-    pl.semaphore_wait(barrier, 46)
+    pl.semaphore_wait(barrier, 49)
 
     sent = []
 
@@ -115,6 +125,15 @@
         lax.fori_loop(0, 31, step, 0)
         sent.append(lambda: wait_bytes(batch, sh_send.at[phase]))
         return lambda: wait_bytes(batch, sh_recv.at[phase])
+
+    def few_spread(phase, batch, src_of, dst, device_of):
+        for i in range(7, 0, -1):
+            copy_to(src_of(i), dst, few_send.at[phase], few_recv.at[phase], device_of(i)).start()
+        sent.append(lambda: wait_bytes(batch, few_send.at[phase]))
+        return lambda: wait_bytes(batch, few_recv.at[phase])
+
+    def chip_dev(i):
+        return (dp_peer(i), s)
 
     def wait_bytes(ref, sem):
         pltpu.make_async_copy(ref, ref, sem).wait()
@@ -253,11 +272,16 @@
     gram = dot_t(block, block).astype(BF16)
     for o in range(16):
         if o < 12:
-            part_send[o, 0:16] = folded[16 * o : 16 * o + 16]
+            part_send[o // 8, o % 8, 0:16] = folded[16 * o : 16 * o + 16]
         else:
-            part_send[o, 0:16] = jnp.zeros((16, 256), BF16)
-        part_send[o, 16:32] = gram[16 * o : 16 * o + 16]
-    part_all[d] = part_send[d]
+            part_send[o // 8, o % 8, 0:16] = jnp.zeros((16, 256), BF16)
+        part_send[o // 8, o % 8, 16:32] = gram[16 * o : 16 * o + 16]
+    place8 = lax.rem(d, 8)
+    part_a[place8] = part_send[:, place8]
+    part_in = few_spread(
+        0, part_a.at[pl.ds(0, 7)], lambda i: part_send.at[:, lax.rem(dp_peer(i), 8)],
+        part_a.at[place8], chip_dev,
+    )
     idx_in()
     ids = idx_all[...].astype(F32)
     for half in range(2):
@@ -271,11 +295,29 @@
         summed_ref[pl.ds(r0, n)] = total
         squares = squares + jnp.sum((total * total).reshape(n // 8, 8, 256), axis=0)
     tile = squares[:, :128] + squares[:, 128:]
-    sq1_mine[...] = tile
-    sq1_all[d] = tile
-    sq1_in = dp_spread(4, sq1_all.at[pl.ds(0, 15)], lambda peer: sq1_mine, sq1_all.at[d])
-
-    part_in = dp_spread(2, part_all.at[pl.ds(0, 15)], lambda peer: part_send.at[peer], part_all.at[d])
+    def share(n, place, tile, device_of):
+        sq_mine[n] = tile
+        sq_all[n, place] = tile
+        arrive = few_spread(
+            2 + n, sq_all.at[n, pl.ds(0, 7)], lambda i: sq_mine.at[n], sq_all.at[n, place],
+            device_of,
+        )
+
+        def total():
+            arrive()
+            return jnp.sum(sq_all[n], axis=0)
+
+        return total
+
+    sq_sum = share(0, place8, tile, chip_dev)
+
+    part_in()
+    half_sum = part_a[0].astype(F32)
+    for o in range(1, 8):
+        half_sum = half_sum + part_a[o].astype(F32)
+    part_sum[...] = half_sum.astype(BF16)
+    other = (lax.rem(d + 8, 16), s)
+    part_b_copy = remote(part_sum.at[1 - zh], part_b, w_send.at[0], w_recv.at[0], other)
 
     owner_row = (tok >> 8).astype(F32)
     owner_line = jnp.broadcast_to(owner_row, (128, 128))
@@ -287,11 +329,7 @@
     find_left = jnp.where(at == place, 1.0, 0.0).astype(BF16)
     find_right = jnp.where(at == place + 8.0, 1.0, 0.0).astype(BF16)
 
-    sq1_in()
-    tile = jnp.sum(sq1_all[...], axis=0)
-    sq2_mine[...] = tile
-    sq2_all[s] = tile
-    sq2_in = sh_spread(1, sq2_all.at[pl.ds(0, 31)], lambda peer: sq2_mine, sq2_all.at[s])
+    sq_sum = share(1, zh * 4 + z, sq_sum(), far_dev)
 
     line, col = iota((512, 256), 0), iota((512, 256), 1)
     to, unit = line >> 4, line & 15
@@ -299,19 +337,15 @@
     match = col == ((to + k) & 15) * 16 + (to >> 4) * 8 + k
     pack_left = jnp.where(match & (unit < 8), 1.0, 0.0).astype(BF16)
     pack_right = jnp.where(match & (unit >= 8), 1.0, 0.0).astype(BF16)
-    part_in()
-    whole = part_all[0].astype(F32)
-    for o in range(1, 16):
-        whole = whole + part_all[o].astype(F32)
-    w_mine[...] = whole.astype(BF16)
-    w_all[d] = whole.astype(BF16)
-    weights_in = dp_spread(3, w_all.at[pl.ds(0, 15)], lambda peer: w_mine, w_all.at[d])
-
+    part_b_copy.wait_recv()
+    w_pair[zh] = (part_sum[zh].astype(F32) + part_b[...].astype(F32)).astype(BF16)
+    w_pair_copy = remote(w_pair.at[zh], w_pair.at[zh], w_send.at[1], w_recv.at[1], other)
+
+    sq_sum = share(2, y, sq_sum(), y_dev)
     for load in loads[6:]:
         load.wait()
 
-    sq2_in()
-    total = jnp.sum(sq2_all[...], axis=0)
+    total = sq_sum()
     total = jnp.sum(jnp.sum(total, axis=0, keepdims=True), axis=1, keepdims=True)
     clip = jnp.minimum(1.0, 0.2 * math.sqrt(TOTAL_ENTRIES) / (jnp.sqrt(total) + 1e-06))
     grad = clip * summed_ref[...]
@@ -326,10 +360,15 @@
     rows_send[...] = found
     rows_all[mine16] = rows_send[mine16]
     rows_in = dp_spread(
-        5,
+        2,
         rows_all.at[pl.ds(0, 240)],
         lambda peer: rows_send.at[pl.ds(pl.multiple_of(peer * 16, 16), 16)],
         rows_all.at[mine16],
+    )
+    w_pair_copy.wait_recv()
+    w_all[:, place8] = w_pair[...]
+    weights_in = few_spread(
+        1, w_all.at[:, pl.ds(0, 7)], lambda i: w_pair, w_all.at[:, place8], chip_dev
     )
     state[0] = new_master
     state[1] = new_m1
@@ -344,14 +383,14 @@
     mine_s = pl.ds(pl.multiple_of(s * 16, 16), 16)
     back_all[mine_s] = back_send[mine_s]
     back_in = sh_spread(
-        2,
+        1,
         back_all.at[pl.ds(0, 496)],
         lambda peer: back_send.at[pl.ds(pl.multiple_of(peer * 16, 16), 16)],
         back_all.at[mine_s],
     )
     weights_in()
-    gram = w_all[:, 16:32, :].reshape(256, 256)
-    folded = w_all[0:12, 0:16, :].reshape(192, 256)
+    gram = w_all[:, :, 16:32, :].reshape(256, 256)
+    folded = w_all[:, :, 0:16, :].reshape(256, 256)[0:192]
     back_in()
     back = back_all[...]
     rows = jnp.concatenate([dot(find_left, back), dot(find_right, back)], axis=1)
@@ -359,10 +398,14 @@
     gathered[s] = (rows * lax.rsqrt(mean_sq + 1e-05)).astype(BF16)
 
     first, last = pl.ds(0, FIRST), pl.ds(FIRST, 128 - FIRST)
+    z_order = (1, 3, 2)
+
+    def z_of(j):
+        return (z, z + 1 - 2 * lax.rem(z, 2), lax.rem(z + 2, 4), 3 - z)[j]
 
     def block_at(step, way, j):
         back_by = (8 - step) if way == 0 else step
-        return lax.rem(y + back_by, 8) * 4 + lax.rem(z + j, 4)
+        return lax.rem(y + back_by, 8) * 4 + z_of(j)
 
     def ring_to(way):
         return y_dev(1 if way == 0 else 7)
@@ -391,10 +434,10 @@
 
     def last_along_z(step, way):
         part = gathered.at[block_at(step, way, 0), last]
-        for k in (2, 1, 3):
+        for j in z_order:
             remote(
-                part, part, zl_send.at[way, step - 1, 4 - k], zl_recv.at[way, step - 1, 4 - k],
-                (d, y * 4 + lax.rem(z + k, 4)),
+                part, part, zl_send.at[way, step - 1, j], zl_recv.at[way, step - 1, j],
+                (d, y * 4 + z_of(j)),
             )
 
     def project(step, way, j):
@@ -405,25 +448,31 @@
         qkv[:, columns] = dot_t(folded, gathered[at]).astype(BF16)
         pltpu.make_async_copy(qkv.at[:, columns], o_q.at[:, columns], out_sem.at[3]).start()
 
+    def own_along_z(rows, n):
+        part = gathered.at[s, rows]
+        for j in z_order:
+            remote(part, part, z_send.at[n, j], z_recv.at[n, j], (d, y * 4 + z_of(j)))
+
+    own_along_z(first, 0)
+    for way in range(2):
+        first_on(0, way, 0)
     for way in range(2):
         last_on(0, way)
-    for k in (2, 1, 3):
-        remote(
-            gathered.at[s], gathered.at[s], z_send.at[4 - k], z_recv.at[4 - k],
-            (d, y * 4 + lax.rem(z + k, 4)),
-        )
-    for j in range(4):
-        if j:
-            wait_bytes(gathered.at[block_at(0, 0, j)], z_recv.at[j])
+    own_along_z(last, 1)
+    project(0, 0, 0)
+    for j in z_order:
+        wait_bytes(gathered.at[block_at(0, 0, j), first], z_recv.at[0, j])
         for way in range(2):
             first_on(0, way, j)
+    for j in z_order:
+        wait_bytes(gathered.at[block_at(0, 0, j), last], z_recv.at[1, j])
         project(0, 0, j)
     for step in (1, 2, 3):
         for way in range(2):
             last_in(step, way)
             last_on(step, way)
             last_along_z(step, way)
-        for j in range(4):
+        for j in (0,) + z_order:
             for way in range(2):
                 first_in(step, way, j)
                 if step < 3 or j // 2 == way:
@@ -438,7 +487,7 @@
     for j in range(4):
         for way in range(2):
             project(3, way, j)
-    for j in range(4):
+    for j in (0, 3, 1, 2):
         first_in(4, j // 2, j)
         project(4, 0, j)
 
@@ -500,14 +549,14 @@
             pltpu.VMEM((256, 128), BF16),
             pltpu.VMEM((256, 256), BF16),
             pltpu.VMEM((256, 256), BF16),
-            pltpu.VMEM((16, 32, 256), BF16),
-            pltpu.VMEM((16, 32, 256), BF16),
+            pltpu.VMEM((2, 8, 32, 256), BF16),
+            pltpu.VMEM((8, 2, 32, 256), BF16),
+            pltpu.VMEM((2, 32, 256), BF16),
             pltpu.VMEM((32, 256), BF16),
-            pltpu.VMEM((16, 32, 256), BF16),
-            pltpu.VMEM((8, 128), F32),
-            pltpu.VMEM((16, 8, 128), F32),
-            pltpu.VMEM((8, 128), F32),
-            pltpu.VMEM((32, 8, 128), F32),
+            pltpu.VMEM((2, 32, 256), BF16),
+            pltpu.VMEM((2, 8, 32, 256), BF16),
+            pltpu.VMEM((3, 8, 128), F32),
+            pltpu.VMEM((3, 8, 8, 128), F32),
             pltpu.VMEM((256, 256), BF16),
             pltpu.VMEM((256, 256), BF16),
             pltpu.VMEM((512, 128), BF16),
@@ -520,9 +569,11 @@
             dma((2, 2)), dma((2, 2)),
             dma((2, 2, 2)), dma((2, 2, 2)),
             dma((2,)), dma((2,)),
-            dma((6,)), dma((6,)),
             dma((3,)), dma((3,)),
-            dma((4,)), dma((4,)),
+            dma((2,)), dma((2,)),
+            dma((5,)), dma((5,)),
+            dma((2,)), dma((2,)),
+            dma((2, 4)), dma((2, 4)),
             dma((2, 4, 4)), dma((2, 4, 4)),
             dma((2, 4)), dma((2, 4)),
             dma((2, 4, 4)), dma((2, 4, 4)),

time: 101 us -> 94.1 us (0.932)
  the two profiles are of different devices: /device:TPU:6 before, /device:TPU:2 now
where the time goes in v3:
time: 94.1 us; the launch traced here: 94 us
  Pallas kernels  93.3 us (99%)
    pallas_call x1, Pallas kernels, body(): pl.pallas_call(kernel, out_shape=(jax.ShapeDtypeStruct((ROWS, 256), F32),...  90.8 us
    pallas_call x1, Pallas kernels, body(): pl.pallas_call(store_kernel, out_shape=tuple((jax.ShapeDtypeStruct(a.shap...  2.57 us

profile of v3, /device:TPU:2, one launch (start us, length us, event | category | flops | bytes accessed | tf_op | source)
XLA Modules:
  0.0 94.0 jit_solution(5931175633022349701)
XLA Ops:
  0.6 90.8 %step.1 = (f32[208,256]{1,0:T(8,128)}, f32[208,256]{1,0:T(8,128)}, f32[208,256]{1,0:T(8,128)}, bf16[192,4096]{1,0:T(8,128)(2,1)}) custom-call(bf16[2,4,2,208,256]{4,3,2,1,0:T(8,128)(2,1)} %bitcast.6, f32[208,256]{1,0:T(8,128)} %master_ref.1, f32[208,256]{1,0:T(8,128)} %m1_ref.1, f32[208,256]{1,0:T(8,128)} %m2_ref.1, bf16[16,4096]{1,0:T(8,128)(2,1)} %proj_hbm.1, ...), custom_call_target="tpu_custom_call" | custom-call | tf_op jit(solution)/shard_map/step/pallas_call | solution.py:522
  91.4 2.6 %store.1 = (f32[208,256]{1,0:T(8,128)}, f32[208,256]{1,0:T(8,128)}, f32[208,256]{1,0:T(8,128)}, bf16[192,4096]{1,0:T(8,128)(2,1)}) custom-call(f32[208,256]{1,0:T(8,128)} %get-tuple-element.12.refs_0_, f32[208,256]{1,0:T(8,128)} %get-tuple-element.13.refs_1_, f32[208,256]{1,0:T(8,128)} %get-tuple-element.14.refs_2_, bf16[192,4096]{1,0:T(8,128)(2,1)} %get-tuple-element.15.refs_3_), custom_call_target="tpu_custom_call" | custom-call | tf_op jit(solution)/shard_map/store/pallas_call | solution.py:596

commit v4 on v3

--- a/solution.py
+++ b/solution.py
@@ -12,6 +12,7 @@
 BF16 = jnp.bfloat16
 ROWS = 208
 FIRST = 96
+FAR_FIRST = sorted(range(1, 32), key=lambda i: -min(i // 4, 8 - i // 4) - (i % 4 > 0))
 PIECES = ((0, 112), (112, 96))
 TOTAL_ENTRIES = 106496 * 256
 
@@ -33,10 +34,11 @@
     o_master, o_m1, o_m2, o_q,
     proj_ref, gain_ref, w_ref, owner_ref, row_ref,
     own, buf_a, buf_b1, buf_b2, send_c, buf_c, state, summed_ref,
-    tok_mine, tok_all, idx_send, idx_all, onehot, proj_all, part_send, part_a, part_sum, part_b, w_pair, w_all,
+    tok_all, idx_send, idx_all, onehot, proj_half, proj_all, part_send, part_a, part_sum, part_b, w_pair, w_all,
     sq_mine, sq_all, rows_send, rows_all, back_send, back_all, gathered, qkv,
     local_sem, out_sem, a_send, a_recv, b1_send, b1_recv, b2_send, b2_recv, c_send, c_recv,
-    dp_send, dp_recv, sh_send, sh_recv, few_send, few_recv, w_send, w_recv, z_send, z_recv, y_send, y_recv, yl_send, yl_recv, zl_send, zl_recv,
+    dp_send, dp_recv, sh_send, sh_recv, few_send, few_recv, w_send, w_recv,
+    tz_send, tz_recv, ty_send, ty_recv, ph_send, ph_recv, z_send, z_recv, y_send, y_recv, yl_send, yl_recv, zl_send, zl_recv,
 ):
     d = lax.axis_index("dp")
     s = lax.axis_index("shard")
@@ -72,25 +74,21 @@
         load.start()
         loads.append(load)
 
+    def z_of(j):
+        return (z, z + 1 - 2 * lax.rem(z, 2), lax.rem(z + 2, 4), 3 - z)[j]
+
+    z_order = (1, 3, 2)
+    half_dev = (lax.rem(d + 8, 16), s)
+
+    def line_dev(j):
+        return (d, y * 4 + z_of(j))
+
     barrier = pltpu.get_barrier_semaphore()
-
-    def greet_dp(i, carry):
-        pl.semaphore_signal(barrier, inc=1, device_id=(dp_peer(1 + i), s), device_id_type=MESH)
-        return carry
-
-    def greet_sh(i, carry):
-        pl.semaphore_signal(barrier, inc=1, device_id=(d, sh_peer(1 + i)), device_id_type=MESH)
-        return carry
-
-    for i in (1, 2, 3, 5, 6, 7):
-
-        @pl.when(lax.rem(z + i, 8) >= 4)
-        def _():
-            pl.semaphore_signal(barrier, inc=1, device_id=far_dev(i), device_id_type=MESH)
-
-    lax.fori_loop(0, 15, greet_dp, 0)
-    lax.fori_loop(0, 31, greet_sh, 0)
-    pl.semaphore_wait(barrier, 49)
+    first_devs = [(d + 1 - 2 * core, s), x_dev(1), x_dev(3), half_dev, y_dev(1), y_dev(7)]
+    first_devs += [line_dev(j) for j in z_order]
+    for dev in first_devs:
+        pl.semaphore_signal(barrier, inc=1, device_id=dev, device_id_type=MESH)
+    pl.semaphore_wait(barrier, len(first_devs))
 
     sent = []
 
@@ -107,22 +105,16 @@
         return copy
 
     def dp_spread(phase, batch, src_of, dst):
-        def step(i, carry):
-            peer = dp_peer(15 - i)
+        for i in range(15, 0, -1):
+            peer = dp_peer(i)
             copy_to(src_of(peer), dst, dp_send.at[phase], dp_recv.at[phase], (peer, s)).start()
-            return carry
-
-        lax.fori_loop(0, 15, step, 0)
         sent.append(lambda: wait_bytes(batch, dp_send.at[phase]))
         return lambda: wait_bytes(batch, dp_recv.at[phase])
 
     def sh_spread(phase, batch, src_of, dst):
-        def step(i, carry):
-            peer = sh_peer(31 - i)
+        for i in FAR_FIRST:
+            peer = sh_peer(i)
             copy_to(src_of(peer), dst, sh_send.at[phase], sh_recv.at[phase], (d, peer)).start()
-            return carry
-
-        lax.fori_loop(0, 31, step, 0)
         sent.append(lambda: wait_bytes(batch, sh_send.at[phase]))
         return lambda: wait_bytes(batch, sh_recv.at[phase])
 
@@ -147,6 +139,32 @@
                 (d + 1 - 2 * core, s),
             )
         )
+
+    loads[0].wait()
+    loads[1].wait()
+    tok = owner_ref[...] * 256 + row_ref[...]
+    tok_all[s] = jnp.broadcast_to(tok, (8, 128))
+    tok_z = [
+        remote(tok_all.at[s], tok_all.at[s], tz_send.at[j], tz_recv.at[j], line_dev(j))
+        for j in z_order
+    ]
+
+    def tok_set(step, way):
+        return tok_all.at[pl.ds(lax.rem(y + ((8 - step) if way == 0 else step), 8) * 4, 4)]
+
+    def tok_on(step, way):
+        part = tok_set(step, way)
+        remote(part, part, ty_send.at[way, step], ty_recv.at[way, step], y_dev(1 if way == 0 else 7))
+
+    def tok_in(step, way):
+        wait_bytes(tok_set(step, way), ty_recv.at[way, step - 1])
+
+    loads[3].wait()
+    half_columns = [pl.ds(pl.multiple_of(h * 2048, 2048), 2048) for h in (zh, 1 - zh)]
+    proj_half_copy = remote(
+        proj_ref.at[:, half_columns[1]], proj_half.at[zh], ph_send.at[0], ph_recv.at[0], half_dev
+    )
+    proj_half[zh] = proj_ref[:, half_columns[0]]
 
     loads[2].wait()
 
@@ -166,14 +184,6 @@
                     b1_send.at[p, zi], b1_recv.at[p, zi], x_dev(k),
                 )
             )
-    loads[0].wait()
-    loads[1].wait()
-    tok = owner_ref[...] * 256 + row_ref[...]
-    tok_tile = jnp.broadcast_to(tok, (8, 128))
-    tok_mine[...] = tok_tile
-    tok_all[s] = tok_tile
-    tokens_in = sh_spread(0, tok_all.at[pl.ds(0, 31)], lambda peer: tok_mine, tok_all.at[s])
-
     a_copies[1].wait_recv()
     a_copies[2].wait_recv()
     add_pair(1, x1)
@@ -188,6 +198,10 @@
     add_pair(0, x1)
     add_pair(1, x3)
 
+    for copy in tok_z:
+        copy.wait_recv()
+    for way in range(2):
+        tok_on(0, way)
     for p, (r0, n) in enumerate(PIECES):
         for zi, xd, k in ((0, x1, 1), (1, x3, 3)):
             b1[2 * p + zi].wait_recv()
@@ -198,22 +212,104 @@
                 own.at[zi, xd, pl.ds(r0, n)], buf_b2.at[zi, 1, pl.ds(r0, n)],
                 b2_send.at[p, zi, 1], b2_recv.at[p, zi, 1], x_dev(k),
             )
-    loads[3].wait()
-    proj_all[pl.ds(pl.multiple_of(d * 16, 16), 16)] = proj_ref[
-        :, pl.ds(pl.multiple_of(d * 256, 256), 256)
-    ]
-    proj_in = dp_spread(
-        0,
-        proj_all.at[pl.ds(0, 240)],
-        lambda peer: proj_ref.at[:, pl.ds(pl.multiple_of(peer * 256, 256), 256)],
-        proj_all.at[pl.ds(pl.multiple_of(d * 16, 16), 16)],
-    )
-
+    for way in range(2):
+        tok_in(1, way)
+        tok_on(1, way)
     a_copies[3].wait_recv()
     for zi in range(2):
         add_pair(zi, x)
 
-    tokens_in()
+    c_copies = []
+    for p, (r0, n) in enumerate(PIECES):
+        for zi in range(2):
+            b2[p, zi, 0].wait_recv()
+            b2[p, zi, 1].wait_recv()
+
+        def total_of(zi):
+            return (
+                own[zi, x, pl.ds(r0, n)].astype(F32)
+                + buf_b2[zi, 0, pl.ds(r0, n)].astype(F32)
+                + buf_b2[zi, 1, pl.ds(r0, n)].astype(F32)
+            )
+
+        send_c[pl.ds(r0, n)] = total_of(1 - zh).astype(BF16)
+        c_copies.append(
+            remote(
+                send_c.at[pl.ds(r0, n)], buf_c.at[pl.ds(r0, n)], c_send.at[p], c_recv.at[p],
+                (lax.rem(d + 8, 16), s),
+            )
+        )
+        summed_ref[pl.ds(r0, n)] = total_of(zh)
+
+    proj_half_copy.wait_recv()
+    place8 = lax.rem(d, 8)
+
+    def half_block(at):
+        return proj_half.at[:, :, pl.ds(pl.multiple_of(at * 256, 256), 256)]
+
+    proj_all[:, place8] = half_block(place8)[...]
+    proj_in = few_spread(
+        5, proj_all.at[:, pl.ds(0, 7)], lambda i: half_block(lax.rem(dp_peer(i), 8)),
+        proj_all.at[:, place8], chip_dev,
+    )
+    for way in range(2):
+        tok_in(2, way)
+        tok_on(2, way)
+    proj_in()
+    loads[4].wait()
+    loads[5].wait()
+    block = proj_all[...].reshape(256, 256)
+    scaled = block.astype(F32) * gain_ref[:, pl.ds(pl.multiple_of(d * 256, 256), 256)]
+    high = scaled.astype(BF16)
+    low = (scaled - high.astype(F32)).astype(BF16)
+    weights = w_ref[...]
+    folded = (dot_t(weights, high) + dot_t(weights, low)).astype(BF16)
+    gram = dot_t(block, block).astype(BF16)
+    for o in range(16):
+        if o < 12:
+            part_send[o // 8, o % 8, 0:16] = folded[16 * o : 16 * o + 16]
+        else:
+            part_send[o // 8, o % 8, 0:16] = jnp.zeros((16, 256), BF16)
+        part_send[o // 8, o % 8, 16:32] = gram[16 * o : 16 * o + 16]
+    part_a[place8] = part_send[:, place8]
+    part_in = few_spread(
+        0, part_a.at[pl.ds(0, 7)], lambda i: part_send.at[:, lax.rem(dp_peer(i), 8)],
+        part_a.at[place8], chip_dev,
+    )
+    for way in range(2):
+        tok_in(3, way)
+    tok_on(3, 0)
+    squares = jnp.zeros((8, 256), F32)
+    for p, (r0, n) in enumerate(PIECES):
+        c_copies[p].wait_recv()
+        total = summed_ref[pl.ds(r0, n)] + buf_c[pl.ds(r0, n)].astype(F32)
+        summed_ref[pl.ds(r0, n)] = total
+        squares = squares + jnp.sum((total * total).reshape(n // 8, 8, 256), axis=0)
+    tile = squares[:, :128] + squares[:, 128:]
+    def share(n, place, tile, device_of):
+        sq_mine[n] = tile
+        sq_all[n, place] = tile
+        arrive = few_spread(
+            2 + n, sq_all.at[n, pl.ds(0, 7)], lambda i: sq_mine.at[n], sq_all.at[n, place],
+            device_of,
+        )
+
+        def total():
+            arrive()
+            return jnp.sum(sq_all[n], axis=0)
+
+        return total
+
+    sq_sum = share(0, place8, tile, chip_dev)
+
+    part_in()
+    half_sum = part_a[0].astype(F32)
+    for o in range(1, 8):
+        half_sum = half_sum + part_a[o].astype(F32)
+    part_sum[...] = half_sum.astype(BF16)
+    part_b_copy = remote(part_sum.at[1 - zh], part_b, w_send.at[0], w_recv.at[0], half_dev)
+
+    tok_in(4, 0)
     tokens = tok_all[:, 0, :]
     member = (tokens >> 8) == s
     row_plus = ((tokens & 255) + 1).astype(F32)
@@ -232,92 +328,11 @@
     mine16 = pl.ds(pl.multiple_of(d * 16, 16), 16)
     idx_all[mine16] = idx_send[mine16]
     idx_in = dp_spread(
-        1,
+        0,
         idx_all.at[pl.ds(0, 240)],
         lambda peer: idx_send.at[pl.ds(pl.multiple_of(peer * 16, 16), 16)],
         idx_all.at[mine16],
     )
-
-    c_copies = []
-    for p, (r0, n) in enumerate(PIECES):
-        for zi in range(2):
-            b2[p, zi, 0].wait_recv()
-            b2[p, zi, 1].wait_recv()
-
-        def total_of(zi):
-            return (
-                own[zi, x, pl.ds(r0, n)].astype(F32)
-                + buf_b2[zi, 0, pl.ds(r0, n)].astype(F32)
-                + buf_b2[zi, 1, pl.ds(r0, n)].astype(F32)
-            )
-
-        send_c[pl.ds(r0, n)] = total_of(1 - zh).astype(BF16)
-        c_copies.append(
-            remote(
-                send_c.at[pl.ds(r0, n)], buf_c.at[pl.ds(r0, n)], c_send.at[p], c_recv.at[p],
-                (lax.rem(d + 8, 16), s),
-            )
-        )
-        summed_ref[pl.ds(r0, n)] = total_of(zh)
-
-    proj_in()
-    loads[4].wait()
-    loads[5].wait()
-    block = proj_all[...]
-    scaled = block.astype(F32) * gain_ref[:, pl.ds(pl.multiple_of(d * 256, 256), 256)]
-    high = scaled.astype(BF16)
-    low = (scaled - high.astype(F32)).astype(BF16)
-    weights = w_ref[...]
-    folded = (dot_t(weights, high) + dot_t(weights, low)).astype(BF16)
-    gram = dot_t(block, block).astype(BF16)
-    for o in range(16):
-        if o < 12:
-            part_send[o // 8, o % 8, 0:16] = folded[16 * o : 16 * o + 16]
-        else:
-            part_send[o // 8, o % 8, 0:16] = jnp.zeros((16, 256), BF16)
-        part_send[o // 8, o % 8, 16:32] = gram[16 * o : 16 * o + 16]
-    place8 = lax.rem(d, 8)
-    part_a[place8] = part_send[:, place8]
-    part_in = few_spread(
-        0, part_a.at[pl.ds(0, 7)], lambda i: part_send.at[:, lax.rem(dp_peer(i), 8)],
-        part_a.at[place8], chip_dev,
-    )
-    idx_in()
-    ids = idx_all[...].astype(F32)
-    for half in range(2):
-        at = (iota((256, 128), 1) + 1 + 128 * half).astype(F32)
-        onehot[:, 128 * half : 128 * half + 128] = jnp.where(ids == at, 1.0, 0.0).astype(BF16)
-
-    squares = jnp.zeros((8, 256), F32)
-    for p, (r0, n) in enumerate(PIECES):
-        c_copies[p].wait_recv()
-        total = summed_ref[pl.ds(r0, n)] + buf_c[pl.ds(r0, n)].astype(F32)
-        summed_ref[pl.ds(r0, n)] = total
-        squares = squares + jnp.sum((total * total).reshape(n // 8, 8, 256), axis=0)
-    tile = squares[:, :128] + squares[:, 128:]
-    def share(n, place, tile, device_of):
-        sq_mine[n] = tile
-        sq_all[n, place] = tile
-        arrive = few_spread(
-            2 + n, sq_all.at[n, pl.ds(0, 7)], lambda i: sq_mine.at[n], sq_all.at[n, place],
-            device_of,
-        )
-
-        def total():
-            arrive()
-            return jnp.sum(sq_all[n], axis=0)
-
-        return total
-
-    sq_sum = share(0, place8, tile, chip_dev)
-
-    part_in()
-    half_sum = part_a[0].astype(F32)
-    for o in range(1, 8):
-        half_sum = half_sum + part_a[o].astype(F32)
-    part_sum[...] = half_sum.astype(BF16)
-    other = (lax.rem(d + 8, 16), s)
-    part_b_copy = remote(part_sum.at[1 - zh], part_b, w_send.at[0], w_recv.at[0], other)
 
     owner_row = (tok >> 8).astype(F32)
     owner_line = jnp.broadcast_to(owner_row, (128, 128))
@@ -339,9 +354,15 @@
     pack_right = jnp.where(match & (unit >= 8), 1.0, 0.0).astype(BF16)
     part_b_copy.wait_recv()
     w_pair[zh] = (part_sum[zh].astype(F32) + part_b[...].astype(F32)).astype(BF16)
-    w_pair_copy = remote(w_pair.at[zh], w_pair.at[zh], w_send.at[1], w_recv.at[1], other)
+    w_pair_copy = remote(w_pair.at[zh], w_pair.at[zh], w_send.at[1], w_recv.at[1], half_dev)
 
     sq_sum = share(2, y, sq_sum(), y_dev)
+    idx_in()
+    ids = idx_all[...].astype(F32)
+    for half in range(2):
+        at = (iota((256, 128), 1) + 1 + 128 * half).astype(F32)
+        onehot[:, 128 * half : 128 * half + 128] = jnp.where(ids == at, 1.0, 0.0).astype(BF16)
+
     for load in loads[6:]:
         load.wait()
 
@@ -360,7 +381,7 @@
     rows_send[...] = found
     rows_all[mine16] = rows_send[mine16]
     rows_in = dp_spread(
-        2,
+        1,
         rows_all.at[pl.ds(0, 240)],
         lambda peer: rows_send.at[pl.ds(pl.multiple_of(peer * 16, 16), 16)],
         rows_all.at[mine16],
@@ -383,7 +404,7 @@
     mine_s = pl.ds(pl.multiple_of(s * 16, 16), 16)
     back_all[mine_s] = back_send[mine_s]
     back_in = sh_spread(
-        1,
+        0,
         back_all.at[pl.ds(0, 496)],
         lambda peer: back_send.at[pl.ds(pl.multiple_of(peer * 16, 16), 16)],
         back_all.at[mine_s],
@@ -398,10 +419,6 @@
     gathered[s] = (rows * lax.rsqrt(mean_sq + 1e-05)).astype(BF16)
 
     first, last = pl.ds(0, FIRST), pl.ds(FIRST, 128 - FIRST)
-    z_order = (1, 3, 2)
-
-    def z_of(j):
-        return (z, z + 1 - 2 * lax.rem(z, 2), lax.rem(z + 2, 4), 3 - z)[j]
 
     def block_at(step, way, j):
         back_by = (8 - step) if way == 0 else step
@@ -543,12 +560,12 @@
             pltpu.VMEM((ROWS, 256), BF16),
             pltpu.VMEM((3, ROWS, 256), F32),
             pltpu.VMEM((ROWS, 256), F32),
-            pltpu.VMEM((8, 128), jnp.int32),
             pltpu.VMEM((32, 8, 128), jnp.int32),
             pltpu.VMEM((256, 128), BF16),
             pltpu.VMEM((256, 128), BF16),
             pltpu.VMEM((256, 256), BF16),
-            pltpu.VMEM((256, 256), BF16),
+            pltpu.VMEM((2, 16, 2048), BF16),
+            pltpu.VMEM((2, 8, 16, 256), BF16),
             pltpu.VMEM((2, 8, 32, 256), BF16),
             pltpu.VMEM((8, 2, 32, 256), BF16),
             pltpu.VMEM((2, 32, 256), BF16),
@@ -566,13 +583,16 @@
             dma((9,)),
             dma((4,)),
             dma((4,)), dma((4,)),
-            dma((2, 2)), dma((2, 2)),
-            dma((2, 2, 2)), dma((2, 2, 2)),
+            dma((len(PIECES), 2)), dma((len(PIECES), 2)),
+            dma((len(PIECES), 2, 2)), dma((len(PIECES), 2, 2)),
+            dma((len(PIECES),)), dma((len(PIECES),)),
             dma((2,)), dma((2,)),
-            dma((3,)), dma((3,)),
+            dma((1,)), dma((1,)),
+            dma((6,)), dma((6,)),
             dma((2,)), dma((2,)),
-            dma((5,)), dma((5,)),
-            dma((2,)), dma((2,)),
+            dma((4,)), dma((4,)),
+            dma((2, 4)), dma((2, 4)),
+            dma((1,)), dma((1,)),
             dma((2, 4)), dma((2, 4)),
             dma((2, 4, 4)), dma((2, 4, 4)),
             dma((2, 4)), dma((2, 4)),

time: 94.1 us -> 90.8 us (0.965)
  the two profiles are of different devices: /device:TPU:2 before, /device:TPU:6 now
where the time goes in v4:
time: 90.8 us; the launch traced here: 90.4 us
  Pallas kernels  89.7 us (99%)
    pallas_call x1, Pallas kernels, body(): pl.pallas_call(kernel, out_shape=(jax.ShapeDtypeStruct((ROWS, 256), F32),...  87.2 us
    pallas_call x1, Pallas kernels, body(): pl.pallas_call(store_kernel, out_shape=tuple((jax.ShapeDtypeStruct(a.shap...  2.57 us

profile of v4, /device:TPU:6, one launch (start us, length us, event | category | flops | bytes accessed | tf_op | source)
XLA Modules:
  0.0 90.4 jit_solution(5435465049053886639)
XLA Ops:
  0.6 87.2 %step.1 = (f32[208,256]{1,0:T(8,128)}, f32[208,256]{1,0:T(8,128)}, f32[208,256]{1,0:T(8,128)}, bf16[192,4096]{1,0:T(8,128)(2,1)}) custom-call(bf16[2,4,2,208,256]{4,3,2,1,0:T(8,128)(2,1)} %bitcast.6, f32[208,256]{1,0:T(8,128)} %master_ref.1, f32[208,256]{1,0:T(8,128)} %m1_ref.1, f32[208,256]{1,0:T(8,128)} %m2_ref.1, bf16[16,4096]{1,0:T(8,128)(2,1)} %proj_hbm.1, ...), custom_call_target="tpu_custom_call" | custom-call | tf_op jit(solution)/shard_map/step/pallas_call | solution.py:539
  87.8 2.6 %store.1 = (f32[208,256]{1,0:T(8,128)}, f32[208,256]{1,0:T(8,128)}, f32[208,256]{1,0:T(8,128)}, bf16[192,4096]{1,0:T(8,128)(2,1)}) custom-call(f32[208,256]{1,0:T(8,128)} %get-tuple-element.12.refs_0_, f32[208,256]{1,0:T(8,128)} %get-tuple-element.13.refs_1_, f32[208,256]{1,0:T(8,128)} %get-tuple-element.14.refs_2_, bf16[192,4096]{1,0:T(8,128)(2,1)} %get-tuple-element.15.refs_3_), custom_call_target="tpu_custom_call" | custom-call | tf_op jit(solution)/shard_map/store/pallas_call | solution.py:616

commit v5 on v4

--- a/solution.py
+++ b/solution.py
@@ -11,7 +11,7 @@
 F32 = jnp.float32
 BF16 = jnp.bfloat16
 ROWS = 208
-FIRST = 96
+FIRST = 80
 FAR_FIRST = sorted(range(1, 32), key=lambda i: -min(i // 4, 8 - i // 4) - (i % 4 > 0))
 PIECES = ((0, 112), (112, 96))
 TOTAL_ENTRIES = 106496 * 256
@@ -91,6 +91,12 @@
     pl.semaphore_wait(barrier, len(first_devs))
 
     sent = []
+
+    def settle(count):
+        for wait in sent[:count]:
+            wait()
+        del sent[:count]
+
 
     def copy_to(src, dst, send_sem, recv_sem, device):
         return pltpu.make_async_remote_copy(
@@ -372,20 +378,20 @@
     grad = clip * summed_ref[...]
     new_m1 = 0.9 * state[1] + 0.1 * grad
     new_m2 = 0.95 * state[2] + 0.05 * grad * grad
-    one = new_m1 / (1.0 - 0.9**10)
-    two = new_m2 / (1.0 - 0.95**10)
+    one = new_m1 * (1.0 / (1.0 - 0.9**10))
+    two = new_m2 * (1.0 / (1.0 - 0.95**10))
     master = state[0]
     new_master = master - 0.01 * (one / (jnp.sqrt(two) + 1e-08) + 0.1 * master)
     table = new_master.astype(BF16)
     found = dot(onehot[:, 0:ROWS], table).astype(BF16)
     rows_send[...] = found
-    rows_all[mine16] = rows_send[mine16]
     rows_in = dp_spread(
         1,
         rows_all.at[pl.ds(0, 240)],
         lambda peer: rows_send.at[pl.ds(pl.multiple_of(peer * 16, 16), 16)],
         rows_all.at[mine16],
     )
+    rows_all[mine16] = rows_send[mine16]
     w_pair_copy.wait_recv()
     w_all[:, place8] = w_pair[...]
     weights_in = few_spread(
@@ -398,17 +404,19 @@
         store = pltpu.make_async_copy(state.at[n], ref, out_sem.at[n])
         store.start()
         sent.append(store.wait)
+    settle(len(sent) - 5)
     rows_in()
     rows = rows_all[...]
     back_send[...] = (dot(pack_left, rows[:, :128]) + dot(pack_right, rows[:, 128:])).astype(BF16)
     mine_s = pl.ds(pl.multiple_of(s * 16, 16), 16)
-    back_all[mine_s] = back_send[mine_s]
     back_in = sh_spread(
         0,
         back_all.at[pl.ds(0, 496)],
         lambda peer: back_send.at[pl.ds(pl.multiple_of(peer * 16, 16), 16)],
         back_all.at[mine_s],
     )
+    back_all[mine_s] = back_send[mine_s]
+    settle(len(sent) - 1)
     weights_in()
     gram = w_all[:, :, 16:32, :].reshape(256, 256)
     folded = w_all[:, :, 0:16, :].reshape(256, 256)[0:192]
@@ -438,8 +446,7 @@
     def last_rows(step, way):
         if step < 3:
             return last
-        half = (128 - FIRST) // 2
-        return pl.ds(FIRST + way * half, half)
+        return pl.ds(FIRST + way * 32, 32 - 16 * way)
 
     def last_on(step, way):
         part = gathered.at[block_at(step, way, 0), last_rows(step, way)]
@@ -483,7 +490,7 @@
             first_on(0, way, j)
     for j in z_order:
         wait_bytes(gathered.at[block_at(0, 0, j), last], z_recv.at[1, j])
-        project(0, 0, j)
+    marks = [len(sent)]
     for step in (1, 2, 3):
         for way in range(2):
             last_in(step, way)
@@ -494,10 +501,16 @@
                 first_in(step, way, j)
                 if step < 3 or j // 2 == way:
                     first_on(step, way, j)
-        if step > 1:
+        if step == 1:
+            for j in z_order:
+                project(0, 0, j)
+        else:
             for j in range(4):
                 for way in range(2):
                     project(step - 1, way, j)
+        if step == 3:
+            settle(marks[1])
+        marks.append(len(sent))
     for way in range(2):
         last_in(4, way)
     last_along_z(4, 0)

time: 90.8 us -> 89.8 us (0.989)
  Pallas kernels: 89.7 us -> 88.6 us
    pallas_call x1, Pallas kernels: 87.2 us -> 86 us  [body(): pl.pallas_call(kernel, out_shape=(jax.ShapeDtypeStruct((ROWS, 256), F32),...]
where the time goes in v5:
time: 89.8 us; the launch traced here: 89.2 us
  Pallas kernels  88.6 us (99%)
    pallas_call x1, Pallas kernels, body(): pl.pallas_call(kernel, out_shape=(jax.ShapeDtypeStruct((ROWS, 256), F32),...  86 us
    pallas_call x1, Pallas kernels, body(): pl.pallas_call(store_kernel, out_shape=tuple((jax.ShapeDtypeStruct(a.shap...  2.57 us

profile of v5, /device:TPU:6, one launch (start us, length us, event | category | flops | bytes accessed | tf_op | source)
XLA Modules:
  0.0 89.2 jit_solution(10549295235116369507)
XLA Ops:
  0.6 86.0 %step.1 = (f32[208,256]{1,0:T(8,128)}, f32[208,256]{1,0:T(8,128)}, f32[208,256]{1,0:T(8,128)}, bf16[192,4096]{1,0:T(8,128)(2,1)}) custom-call(bf16[2,4,2,208,256]{4,3,2,1,0:T(8,128)(2,1)} %bitcast.6, f32[208,256]{1,0:T(8,128)} %master_ref.1, f32[208,256]{1,0:T(8,128)} %m1_ref.1, f32[208,256]{1,0:T(8,128)} %m2_ref.1, bf16[16,4096]{1,0:T(8,128)(2,1)} %proj_hbm.1, ...), custom_call_target="tpu_custom_call" | custom-call | tf_op jit(solution)/shard_map/step/pallas_call | solution.py:552
  86.6 2.6 %store.1 = (f32[208,256]{1,0:T(8,128)}, f32[208,256]{1,0:T(8,128)}, f32[208,256]{1,0:T(8,128)}, bf16[192,4096]{1,0:T(8,128)(2,1)}) custom-call(f32[208,256]{1,0:T(8,128)} %get-tuple-element.12.refs_0_, f32[208,256]{1,0:T(8,128)} %get-tuple-element.13.refs_1_, f32[208,256]{1,0:T(8,128)} %get-tuple-element.14.refs_2_, bf16[192,4096]{1,0:T(8,128)(2,1)} %get-tuple-element.15.refs_3_), custom_call_target="tpu_custom_call" | custom-call | tf_op jit(solution)/shard_map/store/pallas_call | solution.py:629

commit v6 on v5

--- a/solution.py
+++ b/solution.py
@@ -13,7 +13,7 @@
 ROWS = 208
 FIRST = 80
 FAR_FIRST = sorted(range(1, 32), key=lambda i: -min(i // 4, 8 - i // 4) - (i % 4 > 0))
-PIECES = ((0, 112), (112, 96))
+PIECES = ((0, 128), (128, 80))
 TOTAL_ENTRIES = 106496 * 256
 
 
@@ -291,7 +291,7 @@
         total = summed_ref[pl.ds(r0, n)] + buf_c[pl.ds(r0, n)].astype(F32)
         summed_ref[pl.ds(r0, n)] = total
         squares = squares + jnp.sum((total * total).reshape(n // 8, 8, 256), axis=0)
-    tile = squares[:, :128] + squares[:, 128:]
+    tile = jnp.sum(squares[:, :128] + squares[:, 128:], axis=0, keepdims=True)
     def share(n, place, tile, device_of):
         sq_mine[n] = tile
         sq_all[n, place] = tile
@@ -528,7 +528,7 @@
 
 def store_kernel(*refs):
     sources, targets, held, sem = refs[:4], refs[4:8], refs[8:12], refs[12]
-    parts = [(n, slice(None)) for n in range(3)] + [(3, pl.ds(1024 * c, 1024)) for c in range(4)]
+    parts = [(n, slice(None)) for n in range(3)] + [(3, pl.ds(2048 * c, 2048)) for c in range(2)]
     loads = [
         pltpu.make_async_copy(sources[n].at[:, at], held[n].at[:, at], sem.at[0, i])
         for i, (n, at) in enumerate(parts)
@@ -585,8 +585,8 @@
             pltpu.VMEM((32, 256), BF16),
             pltpu.VMEM((2, 32, 256), BF16),
             pltpu.VMEM((2, 8, 32, 256), BF16),
-            pltpu.VMEM((3, 8, 128), F32),
-            pltpu.VMEM((3, 8, 8, 128), F32),
+            pltpu.VMEM((3, 1, 128), F32),
+            pltpu.VMEM((3, 8, 1, 128), F32),
             pltpu.VMEM((256, 256), BF16),
             pltpu.VMEM((256, 256), BF16),
             pltpu.VMEM((512, 128), BF16),
@@ -631,7 +631,7 @@
         out_shape=tuple(jax.ShapeDtypeStruct(a.shape, a.dtype) for a in results),
         in_specs=[pl.BlockSpec(memory_space=pl.ANY)] * 4,
         out_specs=[hbm] * 4,
-        scratch_shapes=[pltpu.VMEM(a.shape, a.dtype) for a in results] + [dma((2, 7))],
+        scratch_shapes=[pltpu.VMEM(a.shape, a.dtype) for a in results] + [dma((2, 5))],
         name="store",
     )(*results)
     return new_master, new_m1, new_m2, qkv_t.T

time: 89.8 us -> 89 us (level)
  Pallas kernels: 88.6 us -> 87.2 us
    pallas_call x1, Pallas kernels: 86 us -> 84.6 us  [body(): pl.pallas_call(kernel, out_shape=(jax.ShapeDtypeStruct((ROWS, 256), F32),...]
where the time goes in v6:
time: 89 us; the launch traced here: 87.9 us
  Pallas kernels  87.2 us (98%)
    pallas_call x1, Pallas kernels, body(): pl.pallas_call(kernel, out_shape=(jax.ShapeDtypeStruct((ROWS, 256), F32),...  84.6 us
    pallas_call x1, Pallas kernels, body(): pl.pallas_call(store_kernel, out_shape=tuple((jax.ShapeDtypeStruct(a.shap...  2.68 us

profile of v6, /device:TPU:6, one launch (start us, length us, event | category | flops | bytes accessed | tf_op | source)
XLA Modules:
  0.0 87.9 jit_solution(12390871115382231190)
XLA Ops:
  0.6 84.6 %step.1 = (f32[208,256]{1,0:T(8,128)}, f32[208,256]{1,0:T(8,128)}, f32[208,256]{1,0:T(8,128)}, bf16[192,4096]{1,0:T(8,128)(2,1)}) custom-call(bf16[2,4,2,208,256]{4,3,2,1,0:T(8,128)(2,1)} %bitcast.6, f32[208,256]{1,0:T(8,128)} %master_ref.1, f32[208,256]{1,0:T(8,128)} %m1_ref.1, f32[208,256]{1,0:T(8,128)} %m2_ref.1, bf16[16,4096]{1,0:T(8,128)(2,1)} %proj_hbm.1, ...), custom_call_target="tpu_custom_call" | custom-call | tf_op jit(solution)/shard_map/step/pallas_call | solution.py:552
  85.2 2.7 %store.1 = (f32[208,256]{1,0:T(8,128)}, f32[208,256]{1,0:T(8,128)}, f32[208,256]{1,0:T(8,128)}, bf16[192,4096]{1,0:T(8,128)(2,1)}) custom-call(f32[208,256]{1,0:T(8,128)} %get-tuple-element.12.refs_0_, f32[208,256]{1,0:T(8,128)} %get-tuple-element.13.refs_1_, f32[208,256]{1,0:T(8,128)} %get-tuple-element.14.refs_2_, bf16[192,4096]{1,0:T(8,128)(2,1)} %get-tuple-element.15.refs_3_), custom_call_target="tpu_custom_call" | custom-call | tf_op jit(solution)/shard_map/store/pallas_call | solution.py:629
